TPU v7x, 32 devices: a whole 2x2x4 slice. The times are simulated.
32 devices in a mesh: groups: 2 (over y), seq: 4 (over z), section: 4 (over x, core).
Axes of the slice: x: 2, y: 2, z: 4, core: 2. Of those that a mesh axis runs over, the one named last changes fastest.
Arguments:
- hidden: bfloat16 [4, 32, 3072], P('section', ('groups', 'seq')), parts along dimension 1, may hold values from -6 to 6
- kv_cache: bfloat16 [4, 4, 32, 2, 3072], P('section', None, ('groups', 'seq')), parts along dimension 2, may hold values from -400 to 400
- w_qkv: bfloat16 [4, 3072, 3, 3072], P('section', None, None, 'seq'), may hold values from -0.109375 to 0.109375
- w_out: bfloat16 [4, 3072, 3072], P('section', None, 'seq'), may hold values from -0.109375 to 0.109375
- norm_gain: float32 [4, 2, 128], P('section'), may hold values from 1 to 2
- modulation: float32 [4, 4, 3, 3072], P('section'), may hold values from -5 to 5
- patch_order: int32 [8], P('groups'), parts along dimension 0, may hold values from 0 to 3, each once
- timestep: int32 [8], P('groups'), parts along dimension 0, may hold values from 0 to 3
Outputs:
- next_hidden: bfloat16 [4, 32, 3072], P('section', ('groups', 'seq')), parts along dimension 1
- fresh_kv: bfloat16 [4, 32, 2, 3072], P('section', ('groups', 'seq')), parts along dimension 1
There are 2 independent parts, one for each index of `groups`. A program takes and returns all parts, laid end to end along the dimension named above; an argument that names none is the same for every part. Nothing has to cross between parts.
Inputs may be any that keep to these rules, and one draw needn't show every extreme that they name: `patch_order`: each section holds a different patch.
All inputs are finite; a program needn't handle non-finite values.
Results may differ from a plain program's by a relative error of at most 0.02.
The roundings to bfloat16 on the way count: a program that leaves them out, or rounds other values in their place, can miss the bound.
Values may be sent and summed in bfloat16 or wider, within the bound.
A program may use at most 64 MiB of HBM per device.

v0:
```python
import math

import jax
import jax.numpy as jnp
from jax import lax
from jax.sharding import PartitionSpec as P


def passed_along(array, axis, by):
    count = lax.axis_size(axis)
    return lax.ppermute(array, axis, [(i, (i + by) % count) for i in range(count)])


def layer_norm(values_in):
    center = values_in - jnp.mean(values_in, axis=-1, keepdims=True)
    spread = jnp.mean(center * center, axis=-1, keepdims=True)
    return center * lax.rsqrt(spread + 1e-06)


def head_norm(values_in, gain):
    square = jnp.mean(values_in * values_in, axis=-1, keepdims=True)
    return values_in * lax.rsqrt(square + 1e-06) * gain


def body(hidden, kv_cache, w_qkv, w_out, norm_gain, modulation, patch_order, timestep):
    section_index = lax.axis_index("section")
    patch_index = lax.dynamic_index_in_dim(patch_order, section_index, 0, keepdims=False)
    step_index = lax.dynamic_index_in_dim(timestep, section_index, 0, keepdims=False)
    modulate = lax.dynamic_index_in_dim(modulation[0], step_index, 0, keepdims=False)
    model_width = hidden.shape[2]
    head_size = norm_gain.shape[2]
    head_count = model_width // head_size
    col_width = w_qkv.shape[3]
    rows_in = hidden[0].astype(jnp.float32)
    own_count = rows_in.shape[0]
    normed = (layer_norm(rows_in) * (1.0 + modulate[1]) + modulate[0]).astype(jnp.bfloat16)
    w_local = w_qkv[0].reshape(model_width, 3 * col_width)
    projected = jnp.dot(
        lax.all_gather(normed, "seq", axis=0, tiled=True),
        w_local,
        preferred_element_type=jnp.float32,
    ).astype(jnp.bfloat16)
    patch_len = projected.shape[0]
    projected = projected.reshape(patch_len, 3, col_width)
    query_cols = lax.all_gather(projected[:, 0], "seq", axis=1, tiled=True)
    kv_rows = lax.all_to_all(projected[:, 1:], "seq", split_axis=0, concat_axis=2, tiled=True)
    queries = head_norm(
        query_cols.astype(jnp.float32).reshape(patch_len, head_count, head_size), norm_gain[0, 0]
    ).astype(jnp.bfloat16)
    key_rows = head_norm(
        kv_rows[:, 0].astype(jnp.float32).reshape(own_count, head_count, head_size), norm_gain[0, 1]
    ).astype(jnp.bfloat16)
    fresh = jnp.stack([key_rows.reshape(own_count, model_width), kv_rows[:, 1]], axis=1)
    zero = jnp.zeros((), jnp.int32)
    local_kv = lax.dynamic_update_slice(kv_cache[0], fresh[None], (patch_index, zero, zero, zero))
    patch_count = local_kv.shape[0]
    local_keys = local_kv[:, :, 0].reshape(patch_count * own_count, head_count, head_size)
    local_values = local_kv[:, :, 1].reshape(patch_count * own_count, head_count, head_size)
    scores = jnp.einsum(
        "thd,shd->hts", queries, local_keys, preferred_element_type=jnp.float32
    ) / math.sqrt(head_size)
    row_top = lax.pmax(jnp.max(scores, axis=-1), "seq")
    weights = jnp.exp(scores - row_top[:, :, None]).astype(jnp.bfloat16)
    denominator = jnp.sum(weights, axis=-1, dtype=jnp.float32).T
    numerator = jnp.einsum(
        "hts,shd->thd", weights, local_values, preferred_element_type=jnp.float32
    ).reshape(patch_len, model_width)
    totals, counts = (
        lax.psum(numerator.astype(jnp.bfloat16), "seq").astype(jnp.float32),
        lax.psum(denominator.astype(jnp.bfloat16), "seq").astype(jnp.float32),
    )
    attention = (totals.reshape(patch_len, head_count, head_size) / counts[:, :, None]).astype(
        jnp.bfloat16
    )
    attention = attention.reshape(patch_len, model_width)
    out_cols = jnp.dot(attention, w_out[0], preferred_element_type=jnp.float32).astype(jnp.bfloat16)
    out_rows = lax.all_to_all(out_cols, "seq", split_axis=0, concat_axis=1, tiled=True)
    block = (rows_in + modulate[2] * out_rows.astype(jnp.float32)).astype(jnp.bfloat16)
    arrived = passed_along(block, "section", 1)
    return (arrived[None], fresh[None])


def solution(mesh):
    return jax.shard_map(
        body,
        mesh=mesh,
        in_specs=(
            P("section", ("groups", "seq"), None),
            P("section", None, ("groups", "seq"), None, None),
            P("section", None, None, "seq"),
            P("section", None, "seq"),
            P("section", None, None),
            P("section", None, None, None),
            P("groups"),
            P("groups"),
        ),
        out_specs=(
            P("section", ("groups", "seq"), None),
            P("section", ("groups", "seq"), None, None),
        ),
        check_vma=False,
    )
```

profile of v0, /device:TPU:1, one launch (start us, length us, event | category | flops | bytes accessed | tf_op | source)
XLA Modules:
  0.0 155.3 jit_solution(8221485039574207923)
XLA Ops:
  7.2 1.2 dynamic_slice.11
  9.7 0.9 convert_reduce_fusion
  10.6 0.9 fusion.15
  12.2 0.9 constant_dynamic-slice_fusion
  13.1 0.8 fusion.21
  13.9 11.9 %all-gather.1 = bf16[4,4,3072]{2,1,0:T(4,128)(2,1)S(1)} all-gather(bf16[1,4,3072]{2,1,0:T(4,128)(2,1)S(1)} %fusion.21), channel_id=1, replica_groups=mesh['groups'=2,'seq'=4,'section'=4] {'seq'}, dimensions={0}, use_global_device_ids=true | all-gather | bytes 122880 | tf_op jit(solution)/shard_map/all_gather | solution.py:39
  25.9 18.6 %copy.27 = bf16[1,3072,3,768]{1,3,2,0:T(8,128)(2,1)} copy(bf16[1,3072,3,768]{3,1,2,0:T(8,128)(2,1)} %param.10) | data formatting | bytes 28311552 | tf_op args[2]
  44.5 0.0 copy-start.2
  44.5 0.0 copy-start.3
  44.5 0.0 copy-start
  44.5 0.0 copy-start.1
  44.5 8.8 %convolution_convert_fusion = bf16[16,2304]{1,0:T(8,128)(2,1)S(1)} fusion(bf16[16,3072]{1,0:T(8,128)(2,1)S(1)} %reshape.88, bf16[3072,2304]{0,1:T(8,128)(2,1)} %bitcast.72), kind=kOutput, calls=%fused_computation.2 | convolution fusion | flops 226529280 | bytes 14327808 | tf_op jit(solution)/shard_map/dot_general | solution.py:38
  53.4 0.1 reshape.77
  53.4 0.7 slice.47
  54.1 3.9 %all-to-all-start = ((bf16[16,2,768]{2,1,0:T(2,128)(2,1)}), bf16[16,2,768]{2,1,0:T(2,128)(2,1)S(1)}, u32[]{:S(2)}, u32[]{:S(2)}) async-start(bf16[16,2,768]{2,1,0:T(2,128)(2,1)} %slice.47), calls=%async_computation | async-start | bytes 98304 | tf_op jit(solution)/shard_map/all_to_all | solution.py:46
  58.0 0.0 all-reduce.2.cloned.1.call-start
  58.0 11.1 %all-gather = bf16[16,1,3072]{2,1,0:T(2,128)(2,1)S(1)} all-gather(bf16[16,1,768]{2,1,0:T(2,128)(2,1)S(1)} %slice.51), channel_id=2, replica_groups=mesh['groups'=2,'seq'=4,'section'=4] {'seq'}, dimensions={2}, use_global_device_ids=true | all-gather | bytes 122880 | tf_op jit(solution)/shard_map/all_gather | solution.py:45
  69.1 0.2 reshape.84
  69.3 0.1 multiply_reduce_fusion
  69.5 0.0 copy-done.2
  69.5 0.1 multiply_convert_fusion
  69.6 0.0 copy-done.3
  69.6 0.6 dynamic_slice.13
  72.2 0.0 all-to-all-done
  72.3 0.1 slice.49
  72.3 0.1 reduce_sum.50
  72.4 0.1 mul.95
  72.5 0.1 multiply_convert_fusion.1
  72.6 0.0 copy-done
  72.6 0.8 constant_dynamic-update-slice_fusion
  73.4 0.9 slice_reduce_fusion.1
  74.3 0.2 fusion.23
  74.5 14.7 %pmax.7 = f32[24,16]{1,0:T(8,128)S(1)} all-reduce(f32[24,16]{1,0:T(8,128)S(1)} %get-tuple-element.11), channel_id=1, replica_groups=mesh['groups'=2,'seq'=4,'section'=4] {'seq'}, use_global_device_ids=true, to_apply=%region_5.6 | all-reduce | flops 384 | bytes 3072 | tf_op jit(solution)/shard_map/pmax | solution.py:62
  89.2 0.2 fusion.2
  89.5 0.6 copy.52
  90.1 0.0 all-reduce.2.cloned.1.call-update
  90.1 0.1 fusion.22
  90.2 0.1 copy.34
  90.3 6.6 %psum.15 = bf16[16,24]{1,0:T(8,128)(2,1)S(1)} all-reduce(bf16[16,24]{1,0:T(8,128)(2,1)S(1)} %bitcast.89), channel_id=1, replica_groups=mesh['groups'=2,'seq'=4,'section'=4] {'seq'}, use_global_device_ids=true, to_apply=%region_8.9 | all-reduce | flops 384 | bytes 1536 | tf_op jit(solution)/shard_map/psum | solution.py:70
  96.9 34.0 %all-reduce.2.cloned.1.call-done = bf16[16,3072]{1,0:T(8,128)(2,1)} async-done(((bf16[16,3072]{1,0:T(8,128)(2,1)}), bf16[16,3072]{1,0:T(8,128)(2,1)}) %all-reduce.2.cloned.1.call-update) | async-done | bytes 98320 | tf_op jit(solution)/shard_map/psum | solution.py:69
  130.9 0.1 div.43
  131.1 3.1 %fusion.3 = bf16[16,768]{1,0:T(8,128)(2,1)S(1)} fusion(bf16[1,3072,768]{2,1,0:T(8,128)(2,1)} %param.11, f32[2,8,24,128]{3,2,1,0:T(8,128)S(1)} %bitcast.76, bf16[16,3072]{1,0:T(8,128)(2,1)} %all-reduce.2.cloned.1.call-done), kind=kOutput, calls=%fused_computation.6 | convolution fusion | flops 75657216 | bytes 5038080 | tf_op jit(solution)/shard_map/dot_general | solution.py:76
  134.2 7.6 %all_to_all.31 = bf16[4,4,768]{2,1,0:T(4,128)(2,1)S(1)} all-to-all(bf16[4,4,768]{2,1,0:T(4,128)(2,1)S(1)} %all_to_all.27), channel_id=1, replica_groups=mesh['groups'=2,'seq'=4,'section'=4] {'seq'}, dimensions={0} | all-to-all | bytes 49152 | tf_op jit(solution)/shard_map/all_to_all | solution.py:77
  141.8 0.0 copy-done.1
  141.8 5.0 %collective-permute-start = (bf16[4,3072]{1,0:T(4,128)(2,1)S(1)}, bf16[4,3072]{1,0:T(4,128)(2,1)S(1)}, u32[]{:S(2)}, u32[]{:S(2)}) collective-permute-start(bf16[4,3072]{1,0:T(4,128)(2,1)S(1)} %fusion.19), channel_id=1, source_target_pairs={{0,1},{1,2},{2,3},{3,0},{4,5},{5,6},{6,7},{7,4},{8,9},{9,10},{10,1... | collective-permute-start | bytes 73736 | tf_op jit(solution)/shard_map/ppermute | solution.py:11
  146.9 0.9 collective-permute-done
  147.8 0.6 copy.58
  (15 shorter events, 0.3 us)
Async XLA Ops:
  44.5 24.9 %copy-start.2 = (f32[1,2,128]{2,1,0:T(2,128)S(1)}, f32[1,2,128]{2,1,0:T(2,128)}, u32[]{:S(2)}) copy-start(f32[1,2,128]{2,1,0:T(2,128)} %param.12) | copy-start | bytes 3076
  44.5 25.1 %copy-start.3 = (s32[4]{0:T(128)S(1)}, s32[4]{0:T(128)}, u32[]{:S(2)}) copy-start(s32[4]{0:T(128)} %param.14) | copy-start | bytes 52
  44.5 28.1 %copy-start = (bf16[1,4,4,2,3072]{4,3,2,1,0:T(2,128)(2,1)S(1)}, bf16[1,4,4,2,3072]{4,3,2,1,0:T(2,128)(2,1)}, u32[]{:S(2)}) copy-start(bf16[1,4,4,2,3072]{4,3,2,1,0:T(2,128)(2,1)} %param.9) | copy-start | bytes 589828
  44.5 97.3 %copy-start.1 = (bf16[1,4,3072]{2,1,0:T(4,128)(2,1)S(1)}, bf16[1,4,3072]{2,1,0:T(4,128)(2,1)}, u32[]{:S(2)}) copy-start(bf16[1,4,3072]{2,1,0:T(4,128)(2,1)} %param.8) | copy-start | bytes 73732
  54.1 18.1 %all-to-all-start = ((bf16[16,2,768]{2,1,0:T(2,128)(2,1)}), bf16[16,2,768]{2,1,0:T(2,128)(2,1)S(1)}, u32[]{:S(2)}, u32[]{:S(2)}) async-start(bf16[16,2,768]{2,1,0:T(2,128)(2,1)} %slice.47), calls=%async_computation | async-start | bytes 98304 | tf_op jit(solution)/shard_map/all_to_all | solution.py:46
  58.0 73.0 %all-reduce.2.cloned.1.call-start = ((), (), s32[]{:S(2)}) async-start(), calls=%async_computation.2 | async-start | bytes 196608 | tf_op jit(solution)/shard_map/psum | solution.py:69
  141.8 6.0 %collective-permute-start = (bf16[4,3072]{1,0:T(4,128)(2,1)S(1)}, bf16[4,3072]{1,0:T(4,128)(2,1)S(1)}, u32[]{:S(2)}, u32[]{:S(2)}) collective-permute-start(bf16[4,3072]{1,0:T(4,128)(2,1)S(1)} %fusion.19), channel_id=1, source_target_pairs={{0,1},{1,2},{2,3},{3,0},{4,5},{5,6},{6,7},{7,4},{8,9},{9,10},{10,1... | collective-permute-start | bytes 73736 | tf_op jit(solution)/shard_map/ppermute | solution.py:11
Sparse Core Ops, SparseCore 0:
  90.2 40.6 all-reduce.1
where the time goes:
time: 158 us; the launch traced here: 155 us
  blocking collectives  51.9 us (33%)
  waiting for transfers between devices  35 us (22%)
  local copies, waits for them, and re-layouts  23.9 us (15%)
  between operations  18.1 us (11%)
  matrix products  12.4 us (8%)
  starting transfers between devices  8.93 us (6%)
  other arithmetic  5.08 us (3%)
    psum x1, waiting for transfers between devices, body(): lax.psum(numerator.astype(jnp.bfloat16), 'seq').astype(jnp.float32)  34 us
    unnamed x11, local copies, waits for them, and re-layouts  19.3 us
    pmax x1, blocking collectives, body(): row_top = lax.pmax(jnp.max(scores, axis=-1), 'seq')  14.7 us
    all_gather x1, blocking collectives, body(): lax.all_gather(normed, 'seq', axis=0, tiled=True)  11.9 us
    all_gather x1, blocking collectives, body(): query_cols = lax.all_gather(projected[:, 0], 'seq', axis=1, tiled=True)  11.1 us
    dot_general x1, matrix products, body(): jnp.dot(lax.all_gather(normed, 'seq', axis=0, tiled=True), w_local, prefe...  8.81 us
    all_to_all x1, blocking collectives, body(): lax.all_to_all(out_cols, 'seq', split_axis=0, concat_axis=1, tiled=True)  7.61 us
    psum x1, blocking collectives, body(): lax.psum(denominator.astype(jnp.bfloat16), 'seq').astype(jnp.float32)  6.61 us
  transfers between devices with their start and end apart: 3, of which 2 were waited for; matrix products, arithmetic and copies ran while one was open for 1% of the time, Pallas kernels for 0%

commit v1 on v0

--- a/solution.py
+++ b/solution.py
@@ -1,8 +1,11 @@
+import functools
 import math
 
 import jax
 import jax.numpy as jnp
 from jax import lax
+from jax.experimental import pallas as pl
+from jax.experimental.pallas import tpu as pltpu
 from jax.sharding import PartitionSpec as P
 
 
@@ -80,9 +83,320 @@
     return (arrived[None], fresh[None])
 
 
+MESH = pl.DeviceIdType.MESH
+
+
+def fused_kernel(
+    n, sections, chunk,
+    patch_ref, step_ref, hidden_hbm, cache_hbm, qkv_hbm, out_hbm, gain_hbm, mod_hbm,
+    next_hbm, fresh_hbm,
+    h_buf, rows_f32, normed, cache_buf, keys, values, w_qkv, w_out, gain, mod,
+    fresh_stage, att_buf, block_stage,
+    sem_qkv, sem_out, sem_small, sem_own, hid_s, hid_r, cache_s, cache_r, fresh_s, fresh_r,
+    att_s, att_r, blk_s, blk_r,
+):
+    f32, bf16 = jnp.float32, jnp.bfloat16
+    me = lax.axis_index("seq")
+    section = lax.axis_index("section")
+    after = lax.rem(section + 1, sections)
+    before = lax.rem(section + sections - 1, sections)
+    tokens, width = h_buf.shape[1], h_buf.shape[2]
+    cols = w_qkv.shape[2]
+    patches = cache_buf.shape[1]
+    head = gain.shape[2]
+    heads = cols // head
+    rows = n * tokens
+    stale = n * patches * tokens
+    parts = width // chunk
+
+    def cols_of(index):
+        return pl.ds(pl.multiple_of(index * cols, head), cols)
+
+    def peer(step):
+        return lax.rem(me + step, n)
+
+    def origin(step):
+        return lax.rem(me + n - step, n)
+
+    own_hidden = pltpu.make_async_copy(hidden_hbm.at[0], h_buf.at[me], sem_own.at[0])
+    own_hidden.start()
+    small = [
+        pltpu.make_async_copy(gain_hbm, gain, sem_small.at[0]),
+        pltpu.make_async_copy(mod_hbm, mod, sem_small.at[1]),
+    ]
+    for copy in small:
+        copy.start()
+    own_cache = pltpu.make_async_copy(
+        cache_hbm.at[0, :, :, :, cols_of(me)], cache_buf.at[me], sem_own.at[1]
+    )
+    own_cache.start()
+    qkv_copies = {}
+    for which in (1, 0, 2):
+        for part in range(parts):
+            span = pl.ds(part * chunk, chunk)
+            qkv_copies[which, part] = pltpu.make_async_copy(
+                qkv_hbm.at[which, span], w_qkv.at[which, span], sem_qkv.at[which, part]
+            )
+
+    barrier = pltpu.get_barrier_semaphore()
+    for step in range(1, n):
+        pl.semaphore_signal(
+            barrier, inc=1, device_id={"seq": peer(step)}, device_id_type=MESH
+        )
+    for index in range(n):
+        pl.semaphore_signal(
+            barrier, inc=1, device_id={"section": before, "seq": index}, device_id_type=MESH
+        )
+    for part in range(parts):
+        qkv_copies[1, part].start()
+    pl.semaphore_wait(barrier, 2 * n - 1)
+
+    sends = []
+
+    def send(src, dst, send_sem, recv_sem, device):
+        copy = pltpu.make_async_remote_copy(
+            src_ref=src, dst_ref=dst, send_sem=send_sem, recv_sem=recv_sem,
+            device_id=device, device_id_type=MESH,
+        )
+        copy.start()
+        sends.append(copy)
+
+    def arrival(dst, send_sem, recv_sem, device):
+        pltpu.make_async_remote_copy(
+            src_ref=dst, dst_ref=dst, send_sem=send_sem, recv_sem=recv_sem,
+            device_id=device, device_id_type=MESH,
+        ).wait_recv()
+
+    for step in range(1, n):
+        send(
+            hidden_hbm.at[0], h_buf.at[me], hid_s.at[step], hid_r.at[me], {"seq": peer(step)}
+        )
+    for step in range(1, n):
+        send(
+            cache_hbm.at[0, :, :, :, cols_of(peer(step))], cache_buf.at[me],
+            cache_s.at[step], cache_r.at[me], {"seq": peer(step)},
+        )
+    for which in (0, 2):
+        for part in range(parts):
+            qkv_copies[which, part].start()
+    out_copies = [
+        pltpu.make_async_copy(out_hbm.at[index], w_out.at[index], sem_out.at[index])
+        for index in range(n)
+    ]
+    for copy in out_copies:
+        copy.start()
+
+    for copy in small:
+        copy.wait()
+    step_index = step_ref[section]
+    chosen = lax.broadcasted_iota(jnp.int32, (mod.shape[1], 1), 0) == step_index
+    shift, scale, gate = (
+        jnp.sum(jnp.where(chosen, mod[which], 0.0), axis=0, keepdims=True) for which in range(3)
+    )
+    block_gate = jnp.sum(
+        jnp.where(chosen, mod[2, :, cols_of(me)], 0.0), axis=0, keepdims=True
+    )
+    own_hidden.wait()
+    for step in range(1, n):
+        arrival(
+            h_buf.at[origin(step)], hid_s.at[step], hid_r.at[origin(step)],
+            {"seq": origin(step)},
+        )
+    for index in range(n):
+        rows_f32[index * tokens : (index + 1) * tokens, :] = h_buf[index].astype(f32)
+    rows_in = rows_f32[...]
+    center = rows_in - jnp.mean(rows_in, axis=-1, keepdims=True)
+    spread = jnp.mean(center * center, axis=-1, keepdims=True)
+    normed[...] = (center * lax.rsqrt(spread + 1e-06) * (1.0 + scale) + shift).astype(bf16)
+
+    own_cache.wait()
+    for step in range(1, n):
+        arrival(
+            cache_buf.at[origin(step)], cache_s.at[step], cache_r.at[origin(step)],
+            {"seq": origin(step)},
+        )
+    per = patches * tokens
+    for index in range(n):
+        pair = cache_buf[index].astype(f32).reshape(per, 2, cols)
+        keys[index * per : (index + 1) * per, :] = pair[:, 0, :].astype(bf16)
+        values[index * per : (index + 1) * per, :] = pair[:, 1, :].astype(bf16)
+
+    def project(which):
+        total = jnp.zeros((rows, cols), f32)
+        for part in range(parts):
+            qkv_copies[which, part].wait()
+            span = slice(part * chunk, (part + 1) * chunk)
+            total += jnp.dot(normed[:, span], w_qkv[which, span, :], preferred_element_type=f32)
+        return total.astype(bf16)
+
+    def head_norms(projected, which):
+        done = []
+        for index in range(heads):
+            vector = projected[:, index * head : (index + 1) * head].astype(f32)
+            square = jnp.mean(vector * vector, axis=-1, keepdims=True)
+            done.append((vector * lax.rsqrt(square + 1e-06) * gain[0, which : which + 1, :]).astype(bf16))
+        return done
+
+    fresh_keys = head_norms(project(1), 1)
+    for index in range(heads):
+        keys[stale:, index * head : (index + 1) * head] = fresh_keys[index]
+    queries = head_norms(project(0), 0)
+
+    count = stale + rows
+    column = lax.broadcasted_iota(jnp.int32, (1, count), 1)
+    is_cache = column < stale
+    in_patch = lax.rem(column // tokens, patches)
+    replaced = jnp.logical_and(is_cache, in_patch == patch_ref[section])
+    group = jnp.where(is_cache, column // per, (column - stale) // tokens)
+    row_group = lax.broadcasted_iota(jnp.int32, (n * rows, 1), 0) // rows
+    same_group = row_group == group
+    weights, counts = [], []
+    for index in range(heads):
+        scores = lax.dot_general(
+            queries[index], keys[:, index * head : (index + 1) * head],
+            (((1,), (1,)), ((), ())), preferred_element_type=f32,
+        ) * (1.0 / math.sqrt(head))
+        scores = jnp.where(replaced, -jnp.inf, scores)
+        top = jnp.max(scores, axis=-1, keepdims=True)
+        weight = jnp.exp(scores - top).astype(bf16).astype(f32)
+        grouped = jnp.where(same_group, jnp.concatenate([weight] * n, axis=0), 0.0)
+        partial = jnp.sum(grouped, axis=-1, keepdims=True).astype(bf16).astype(f32)
+        counts.append(sum(partial[i * rows : (i + 1) * rows] for i in range(n)))
+        weights.append(grouped.astype(bf16))
+
+    fresh_values = project(2)
+    values[stale:, :] = fresh_values
+    for index in range(heads):
+        span = slice(index * head, (index + 1) * head)
+        partial = jnp.dot(weights[index], values[:, span], preferred_element_type=f32)
+        partial = partial.astype(bf16).astype(f32)
+        numerator = sum(partial[i * rows : (i + 1) * rows] for i in range(n))
+        att_buf[me, :, span] = (numerator / counts[index]).astype(bf16)
+    for step in range(1, n):
+        send(
+            att_buf.at[me], att_buf.at[me], att_s.at[step], att_r.at[me], {"seq": peer(step)}
+        )
+
+    keys_f32 = keys[stale:, :].astype(f32)
+    values_f32 = fresh_values.astype(f32)
+    for index in range(n):
+        span = slice(index * tokens, (index + 1) * tokens)
+        which = lax.broadcasted_iota(jnp.int32, (tokens, 2, cols), 1)
+        fresh_stage[index] = jnp.where(
+            which == 0, keys_f32[span][:, None, :], values_f32[span][:, None, :]
+        ).astype(bf16)
+    own_fresh = pltpu.make_async_copy(
+        fresh_stage.at[me], fresh_hbm.at[0, :, :, cols_of(me)], sem_own.at[2]
+    )
+    own_fresh.start()
+    for step in range(1, n):
+        send(
+            fresh_stage.at[peer(step)], fresh_hbm.at[0, :, :, cols_of(me)],
+            fresh_s.at[step], fresh_r.at[me], {"seq": peer(step)},
+        )
+
+    for copy in out_copies:
+        copy.wait()
+    total = jnp.dot(att_buf[me], w_out[me], preferred_element_type=f32)
+    for step in range(1, n):
+        source = origin(step)
+        arrival(att_buf.at[source], att_s.at[step], att_r.at[source], {"seq": source})
+        total += jnp.dot(att_buf[source], w_out[source], preferred_element_type=f32)
+    attn_out = total.astype(bf16).astype(f32)
+    block = rows_f32[:, cols_of(me)] + block_gate * attn_out
+    for index in range(n):
+        block_stage[index] = block[index * tokens : (index + 1) * tokens].astype(bf16)
+    for index in range(n):
+        send(
+            block_stage.at[index], next_hbm.at[0, :, cols_of(me)],
+            blk_s.at[index], blk_r.at[me], {"section": after, "seq": index},
+        )
+    own_fresh.wait()
+    for step in range(1, n):
+        source = origin(step)
+        arrival(
+            fresh_hbm.at[0, :, :, cols_of(source)], fresh_s.at[step], fresh_r.at[source],
+            {"seq": source},
+        )
+    for index in range(n):
+        arrival(
+            next_hbm.at[0, :, cols_of(index)], blk_s.at[index], blk_r.at[index],
+            {"section": before, "seq": index},
+        )
+    for copy in sends:
+        copy.wait_send()
+
+
+def fused(hidden, kv_cache, w_qkv, w_out, norm_gain, modulation, patch_order, timestep):
+    n = lax.axis_size("seq")
+    sections = lax.axis_size("section")
+    tokens, width = hidden.shape[1:]
+    patches = kv_cache.shape[1]
+    cols = w_qkv.shape[3]
+    rows = n * tokens
+    stale = n * patches * tokens
+    chunk = width // 3 if width % 48 == 0 else width
+    parts = width // chunk
+    bf16, f32 = jnp.bfloat16, jnp.float32
+    anywhere = pl.BlockSpec(memory_space=pl.ANY)
+    scalars = pl.BlockSpec(memory_space=pltpu.SMEM)
+    dma = pltpu.SemaphoreType.DMA
+    return pl.pallas_call(
+        functools.partial(fused_kernel, n, sections, chunk),
+        out_shape=(
+            jax.ShapeDtypeStruct(hidden.shape, bf16),
+            jax.ShapeDtypeStruct((1, tokens, 2, width), bf16),
+        ),
+        in_specs=[scalars] * 2 + [anywhere] * 6,
+        out_specs=(anywhere, anywhere),
+        scratch_shapes=[
+            pltpu.VMEM((n, tokens, width), bf16),
+            pltpu.VMEM((rows, width), f32),
+            pltpu.VMEM((rows, width), bf16),
+            pltpu.VMEM((n, patches, tokens, 2, cols), bf16),
+            pltpu.VMEM((stale + rows, cols), bf16),
+            pltpu.VMEM((stale + rows, cols), bf16),
+            pltpu.VMEM((3, width, cols), bf16),
+            pltpu.VMEM((n, cols, cols), bf16),
+            pltpu.VMEM(norm_gain.shape, f32),
+            pltpu.VMEM((3, modulation.shape[1], width), f32),
+            pltpu.VMEM((n, tokens, 2, cols), bf16),
+            pltpu.VMEM((n, rows, cols), bf16),
+            pltpu.VMEM((n, tokens, cols), bf16),
+            dma((3, parts)),
+            dma((n,)),
+            dma((2,)),
+            dma((3,)),
+        ]
+        + [dma((n,))] * 10,
+        compiler_params=pltpu.CompilerParams(
+            collective_id=0, has_side_effects=True, vmem_limit_bytes=50 * 2**20
+        ),
+    )(
+        patch_order,
+        timestep,
+        hidden,
+        kv_cache,
+        jnp.transpose(w_qkv[0], (1, 0, 2)),
+        w_out[0].reshape(n, cols, cols),
+        norm_gain,
+        jnp.transpose(modulation[0], (1, 0, 2)),
+    )
+
+
+def block_step(*arrays):
+    hidden, w_qkv, norm_gain = arrays[0], arrays[2], arrays[4]
+    lanes = norm_gain.shape[2]
+    whole_heads = lanes % 128 == 0 and w_qkv.shape[3] % lanes == 0
+    whole_tiles = lax.axis_size("seq") * hidden.shape[1] % 16 == 0
+    if whole_heads and whole_tiles and lax.axis_size("seq") > 1 and lax.axis_size("section") > 1:
+        return fused(*arrays)
+    return body(*arrays)
+
+
 def solution(mesh):
     return jax.shard_map(
-        body,
+        block_step,
         mesh=mesh,
         in_specs=(
             P("section", ("groups", "seq"), None),

time: 158 us -> 35.3 us (0.22); the launches traced: 155 us -> 35 us
  blocking collectives: 51.9 us -> 0 us
  waiting for transfers between devices: 35 us -> 0 us
  Pallas kernels: 0 us -> 28.5 us
  local copies, waits for them, and re-layouts: 23.9 us -> 5.78 us
  between operations: 18.1 us -> 0.65 us
  matrix products: 12.4 us -> 0 us
  starting transfers between devices: 8.93 us -> 0 us
  other arithmetic: 5.08 us -> 0 us
    psum x1 -> x0, waiting for transfers between devices: 34 us -> none  [body(): lax.psum(numerator.astype(jnp.bfloat16), 'seq').astype(jnp.float32)]
    pallas_call x0 -> x1, Pallas kernels: none -> 28.5 us  [fused(): pl.pallas_call(functools.partial(fused_kernel, n, sections, chunk), out_s...]
    all_gather x2 -> x0, blocking collectives: 23 us -> none  [the longest x1 11.9 us: body(): lax.all_gather(normed, 'seq', axis=0, tiled=True)]
    pmax x1 -> x0, blocking collectives: 14.7 us -> none  [body(): row_top = lax.pmax(jnp.max(scores, axis=-1), 'seq')]
    unnamed x11 -> x14, local copies, waits for them, and re-layouts: 19.3 us -> 5.78 us
    dot_general x4 -> x0, matrix products: 12.4 us -> none  [the longest x1 8.81 us: body(): jnp.dot(lax.all_gather(normed, 'seq', axis=0, tiled=True), w_local, prefe...]
    all_to_all x1 -> x0, blocking collectives: 7.61 us -> none  [body(): lax.all_to_all(out_cols, 'seq', split_axis=0, concat_axis=1, tiled=True)]
    psum x1 -> x0, blocking collectives: 6.61 us -> none  [body(): lax.psum(denominator.astype(jnp.bfloat16), 'seq').astype(jnp.float32)]
  transfers between devices with their start and end apart: 3 -> 0, of which waited for: 2 -> 0; matrix products, arithmetic and copies ran while one was open for 1% -> 0% of each run, Pallas kernels for 0% -> 0%
where the time goes in v1:
time: 35.3 us; the launch traced here: 35 us
  Pallas kernels  28.5 us (81%)
  local copies, waits for them, and re-layouts  5.78 us (16%)
  between operations  0.65 us (2%)
    pallas_call x1, Pallas kernels, fused(): pl.pallas_call(functools.partial(fused_kernel, n, sections, chunk), out_s...  28.5 us
    unnamed x14, local copies, waits for them, and re-layouts  5.78 us

profile of v1, /device:TPU:1, one launch (start us, length us, event | category | flops | bytes accessed | tf_op | source)
XLA Modules:
  0.0 35.0 jit_solution(5193442164390450508)
XLA Ops:
  0.6 0.0 copy-start
  0.6 0.9 %copy-done = bf16[1,4,4,2,3072]{4,3,2,1,0:T(2,128)(2,1)S(1)} copy-done((bf16[1,4,4,2,3072]{4,3,2,1,0:T(2,128)(2,1)S(1)}, bf16[1,4,4,2,3072]{4,3,2,1,0:T(2,128)(2,1)}, u32[]{:S(2)}) %copy-start) | copy-done | bytes 196632
  1.6 0.0 copy-start.1
  1.6 0.9 %copy-done.1 = f32[1,4,3,3072]{3,1,2,0:T(4,128)S(1)} copy-done((f32[1,4,3,3072]{3,1,2,0:T(4,128)S(1)}, f32[1,4,3,3072]{3,1,2,0:T(4,128)}, u32[]{:S(2)}) %copy-start.1) | copy-done | bytes 147480
  2.5 0.0 copy-start.2
  2.5 0.7 %copy-done.2 = bf16[1,4,3072]{2,1,0:T(4,128)(2,1)S(1)} copy-done((bf16[1,4,3072]{2,1,0:T(4,128)(2,1)S(1)}, bf16[1,4,3072]{2,1,0:T(4,128)(2,1)}, u32[]{:S(2)}) %copy-start.2) | copy-done | bytes 24600
  3.2 0.0 copy-start.3
  3.2 0.7 %copy-done.3 = f32[1,2,128]{2,1,0:T(2,128)S(1)} copy-done((f32[1,2,128]{2,1,0:T(2,128)S(1)}, f32[1,2,128]{2,1,0:T(2,128)}, u32[]{:S(2)}) %copy-start.3) | copy-done | bytes 1048
  3.9 0.0 copy-start.4
  3.9 0.7 %copy-done.4 = s32[4]{0:T(128)S(1)} copy-done((s32[4]{0:T(128)S(1)}, s32[4]{0:T(128)}, u32[]{:S(2)}) %copy-start.4) | copy-done | bytes 40
  4.5 0.0 copy-start.5
  4.5 0.7 %copy-done.5 = s32[4]{0:T(128)S(1)} copy-done((s32[4]{0:T(128)S(1)}, s32[4]{0:T(128)}, u32[]{:S(2)}) %copy-start.5) | copy-done | bytes 40
  5.2 28.5 %shard_map.95 = (bf16[1,4,3072]{2,1,0:T(4,128)(2,1)S(1)}, bf16[1,4,2,3072]{3,2,1,0:T(2,128)(2,1)S(1)}) custom-call(s32[4]{0:T(128)S(1)} %copy-done.4, s32[4]{0:T(128)S(1)} %copy-done.5, bf16[1,4,3072]{2,1,0:T(4,128)(2,1)S(1)} %copy-done.2, bf16[1,4,4,2,3072]{4,3,2,1,0:T(2,128)(2,1)S(1)} %copy-done, bf16[3,3072,768]{2,1,0:T(8,128)(2,1)} %bitcast.8, ...), custom_call_target="tpu_custom_call" | custom-call | tf_op jit(solution)/shard_map/pallas_call | solution.py:344
  33.7 0.6 %copy.12 = bf16[1,4,3072]{2,1,0:T(4,128)(2,1)} copy(bf16[1,4,3072]{2,1,0:T(4,128)(2,1)S(1)} %get-tuple-element.4) | data formatting | bytes 49152
  34.3 0.6 %copy.13 = bf16[1,4,2,3072]{3,2,1,0:T(2,128)(2,1)} copy(bf16[1,4,2,3072]{3,2,1,0:T(2,128)(2,1)S(1)} %get-tuple-element.5) | data formatting | bytes 98304
Async XLA Ops:
  0.6 0.9 %copy-start = (bf16[1,4,4,2,3072]{4,3,2,1,0:T(2,128)(2,1)S(1)}, bf16[1,4,4,2,3072]{4,3,2,1,0:T(2,128)(2,1)}, u32[]{:S(2)}) copy-start(bf16[1,4,4,2,3072]{4,3,2,1,0:T(2,128)(2,1)} %cache_hbm.1) | copy-start | bytes 589828
  1.6 0.9 %copy-start.1 = (f32[1,4,3,3072]{3,1,2,0:T(4,128)S(1)}, f32[1,4,3,3072]{3,1,2,0:T(4,128)}, u32[]{:S(2)}) copy-start(f32[1,4,3,3072]{3,1,2,0:T(4,128)} %param.13) | copy-start | bytes 442372
  2.5 0.7 %copy-start.2 = (bf16[1,4,3072]{2,1,0:T(4,128)(2,1)S(1)}, bf16[1,4,3072]{2,1,0:T(4,128)(2,1)}, u32[]{:S(2)}) copy-start(bf16[1,4,3072]{2,1,0:T(4,128)(2,1)} %hidden_hbm.1) | copy-start | bytes 73732
  3.2 0.7 %copy-start.3 = (f32[1,2,128]{2,1,0:T(2,128)S(1)}, f32[1,2,128]{2,1,0:T(2,128)}, u32[]{:S(2)}) copy-start(f32[1,2,128]{2,1,0:T(2,128)} %gain_hbm.1) | copy-start | bytes 3076
  3.9 0.7 %copy-start.4 = (s32[4]{0:T(128)S(1)}, s32[4]{0:T(128)}, u32[]{:S(2)}) copy-start(s32[4]{0:T(128)} %patch_ref.1) | copy-start | bytes 52
  4.5 0.7 %copy-start.5 = (s32[4]{0:T(128)S(1)}, s32[4]{0:T(128)}, u32[]{:S(2)}) copy-start(s32[4]{0:T(128)} %step_ref.1) | copy-start | bytes 52

commit v2 on v1

--- a/solution.py
+++ b/solution.py
@@ -88,67 +88,84 @@
 
 def fused_kernel(
     n, sections, chunk,
-    patch_ref, step_ref, hidden_hbm, cache_hbm, qkv_hbm, out_hbm, gain_hbm, mod_hbm,
+    patch_hbm, step_hbm, hidden_hbm, cache_hbm, qkv_hbm, out_hbm, gain_hbm, mod_hbm,
     next_hbm, fresh_hbm,
-    h_buf, rows_f32, normed, cache_buf, keys, values, w_qkv, w_out, gain, mod,
-    fresh_stage, att_buf, block_stage,
-    sem_qkv, sem_out, sem_small, sem_own, hid_s, hid_r, cache_s, cache_r, fresh_s, fresh_r,
-    att_s, att_r, blk_s, blk_r,
+    own_rows, hid_cols, norm_buf, rows_f32, own_cache, cache_stage, keys, values, w_qkv, w_out,
+    gain, mod, patch, step_at, fresh_stage, att_buf, block_stage,
+    sem_qkv, sem_out, sem_small, norm_s, norm_r, hid_s, hid_r, key_s, key_r, value_s, value_r,
+    fresh_s, fresh_r, att_s, att_r, blk_s, blk_r,
 ):
     f32, bf16 = jnp.float32, jnp.bfloat16
     me = lax.axis_index("seq")
     section = lax.axis_index("section")
     after = lax.rem(section + 1, sections)
     before = lax.rem(section + sections - 1, sections)
-    tokens, width = h_buf.shape[1], h_buf.shape[2]
+    tokens, width = own_rows.shape
     cols = w_qkv.shape[2]
-    patches = cache_buf.shape[1]
+    patches = own_cache.shape[0]
     head = gain.shape[2]
     heads = cols // head
     rows = n * tokens
-    stale = n * patches * tokens
+    per = patches * tokens
+    stale = n * per
     parts = width // chunk
 
     def cols_of(index):
         return pl.ds(pl.multiple_of(index * cols, head), cols)
 
+    def per_of(index):
+        return pl.ds(pl.multiple_of(index * per, per), per)
+
     def peer(step):
         return lax.rem(me + step, n)
 
     def origin(step):
         return lax.rem(me + n - step, n)
 
-    own_hidden = pltpu.make_async_copy(hidden_hbm.at[0], h_buf.at[me], sem_own.at[0])
-    own_hidden.start()
+    barrier = pltpu.get_barrier_semaphore()
+    for step in range(1, n):
+        pl.semaphore_signal(
+            barrier, inc=1, device_id={"seq": peer(step)}, device_id_type=MESH
+        )
+    for index in range(n):
+        pl.semaphore_signal(
+            barrier, inc=1, device_id={"section": before, "seq": index}, device_id_type=MESH
+        )
     small = [
-        pltpu.make_async_copy(gain_hbm, gain, sem_small.at[0]),
-        pltpu.make_async_copy(mod_hbm, mod, sem_small.at[1]),
+        pltpu.make_async_copy(src, dst, sem_small.at[place])
+        for place, (src, dst) in enumerate(
+            (
+                (hidden_hbm.at[0], own_rows),
+                (mod_hbm, mod),
+                (step_hbm, step_at),
+                (patch_hbm, patch),
+                (gain_hbm, gain),
+                (cache_hbm.at[0], own_cache),
+            )
+        )
     ]
     for copy in small:
         copy.start()
-    own_cache = pltpu.make_async_copy(
-        cache_hbm.at[0, :, :, :, cols_of(me)], cache_buf.at[me], sem_own.at[1]
-    )
-    own_cache.start()
     qkv_copies = {}
     for which in (1, 0, 2):
         for part in range(parts):
             span = pl.ds(part * chunk, chunk)
-            qkv_copies[which, part] = pltpu.make_async_copy(
+            copy = pltpu.make_async_copy(
                 qkv_hbm.at[which, span], w_qkv.at[which, span], sem_qkv.at[which, part]
             )
-
-    barrier = pltpu.get_barrier_semaphore()
-    for step in range(1, n):
-        pl.semaphore_signal(
-            barrier, inc=1, device_id={"seq": peer(step)}, device_id_type=MESH
-        )
-    for index in range(n):
-        pl.semaphore_signal(
-            barrier, inc=1, device_id={"section": before, "seq": index}, device_id_type=MESH
-        )
-    for part in range(parts):
-        qkv_copies[1, part].start()
+            copy.start()
+            qkv_copies[which, part] = copy
+
+    for copy in small[:3]:
+        copy.wait()
+    chosen = lax.broadcasted_iota(jnp.int32, (mod.shape[1], 1), 0) == step_at[section]
+    shift, scale = (
+        jnp.sum(jnp.where(chosen, mod[which], 0.0), axis=0, keepdims=True) for which in range(2)
+    )
+    rows_in = own_rows[...].astype(f32)
+    center = rows_in - jnp.mean(rows_in, axis=-1, keepdims=True)
+    spread = jnp.mean(center * center, axis=-1, keepdims=True)
+    norm_buf[me] = (center * lax.rsqrt(spread + 1e-06) * (1.0 + scale) + shift).astype(bf16)
     pl.semaphore_wait(barrier, 2 * n - 1)
 
     sends = []
@@ -168,17 +185,30 @@
         ).wait_recv()
 
     for step in range(1, n):
+        send(norm_buf.at[me], norm_buf.at[me], norm_s.at[step], norm_r.at[me], {"seq": peer(step)})
+
+    for copy in small[3:]:
+        copy.wait()
+    pair = own_cache[...].astype(f32).reshape(per, 2, width)
+    for which in range(2):
+        split = pair[:, which, :].astype(bf16)
+        for index in range(n):
+            cache_stage[which, index] = split[:, index * cols : (index + 1) * cols]
+    for which, (into, send_sem, recv_sem) in enumerate(
+        ((keys, key_s, key_r), (values, value_s, value_r))
+    ):
+        for step in range(1, n):
+            send(
+                cache_stage.at[which, peer(step)], into.at[per_of(me)],
+                send_sem.at[step], recv_sem.at[me], {"seq": peer(step)},
+            )
+        into[per_of(me), :] = cache_stage[which, me]
+    for step in range(1, n):
         send(
-            hidden_hbm.at[0], h_buf.at[me], hid_s.at[step], hid_r.at[me], {"seq": peer(step)}
-        )
-    for step in range(1, n):
-        send(
-            cache_hbm.at[0, :, :, :, cols_of(peer(step))], cache_buf.at[me],
-            cache_s.at[step], cache_r.at[me], {"seq": peer(step)},
-        )
-    for which in (0, 2):
-        for part in range(parts):
-            qkv_copies[which, part].start()
+            own_rows.at[:, cols_of(peer(step))], hid_cols.at[me], hid_s.at[step], hid_r.at[me],
+            {"seq": peer(step)},
+        )
+    hid_cols[me] = own_rows[:, cols_of(me)]
     out_copies = [
         pltpu.make_async_copy(out_hbm.at[index], w_out.at[index], sem_out.at[index])
         for index in range(n)
@@ -186,40 +216,12 @@
     for copy in out_copies:
         copy.start()
 
-    for copy in small:
-        copy.wait()
-    step_index = step_ref[section]
-    chosen = lax.broadcasted_iota(jnp.int32, (mod.shape[1], 1), 0) == step_index
-    shift, scale, gate = (
-        jnp.sum(jnp.where(chosen, mod[which], 0.0), axis=0, keepdims=True) for which in range(3)
-    )
-    block_gate = jnp.sum(
-        jnp.where(chosen, mod[2, :, cols_of(me)], 0.0), axis=0, keepdims=True
-    )
-    own_hidden.wait()
-    for step in range(1, n):
-        arrival(
-            h_buf.at[origin(step)], hid_s.at[step], hid_r.at[origin(step)],
-            {"seq": origin(step)},
-        )
-    for index in range(n):
-        rows_f32[index * tokens : (index + 1) * tokens, :] = h_buf[index].astype(f32)
-    rows_in = rows_f32[...]
-    center = rows_in - jnp.mean(rows_in, axis=-1, keepdims=True)
-    spread = jnp.mean(center * center, axis=-1, keepdims=True)
-    normed[...] = (center * lax.rsqrt(spread + 1e-06) * (1.0 + scale) + shift).astype(bf16)
-
-    own_cache.wait()
-    for step in range(1, n):
-        arrival(
-            cache_buf.at[origin(step)], cache_s.at[step], cache_r.at[origin(step)],
-            {"seq": origin(step)},
-        )
-    per = patches * tokens
-    for index in range(n):
-        pair = cache_buf[index].astype(f32).reshape(per, 2, cols)
-        keys[index * per : (index + 1) * per, :] = pair[:, 0, :].astype(bf16)
-        values[index * per : (index + 1) * per, :] = pair[:, 1, :].astype(bf16)
+    for step in range(1, n):
+        source = origin(step)
+        arrival(norm_buf.at[source], norm_s.at[step], norm_r.at[source], {"seq": source})
+    for index in range(n):
+        rows_f32[index * tokens : (index + 1) * tokens, :] = norm_buf[index].astype(f32)
+    normed = rows_f32[...].astype(bf16)
 
     def project(which):
         total = jnp.zeros((rows, cols), f32)
@@ -234,23 +236,27 @@
         for index in range(heads):
             vector = projected[:, index * head : (index + 1) * head].astype(f32)
             square = jnp.mean(vector * vector, axis=-1, keepdims=True)
-            done.append((vector * lax.rsqrt(square + 1e-06) * gain[0, which : which + 1, :]).astype(bf16))
+            normal = vector * lax.rsqrt(square + 1e-06) * gain[0, which : which + 1, :]
+            done.append(normal.astype(bf16))
         return done
 
-    fresh_keys = head_norms(project(1), 1)
-    for index in range(heads):
-        keys[stale:, index * head : (index + 1) * head] = fresh_keys[index]
+    fresh_keys = jnp.concatenate(head_norms(project(1), 1), axis=1)
+    keys[stale:, :] = fresh_keys
     queries = head_norms(project(0), 0)
 
+    for step in range(1, n):
+        source = origin(step)
+        arrival(keys.at[per_of(source)], key_s.at[step], key_r.at[source], {"seq": source})
+        arrival(values.at[per_of(source)], value_s.at[step], value_r.at[source], {"seq": source})
     count = stale + rows
     column = lax.broadcasted_iota(jnp.int32, (1, count), 1)
     is_cache = column < stale
     in_patch = lax.rem(column // tokens, patches)
-    replaced = jnp.logical_and(is_cache, in_patch == patch_ref[section])
+    replaced = jnp.logical_and(is_cache, in_patch == patch[section])
     group = jnp.where(is_cache, column // per, (column - stale) // tokens)
     row_group = lax.broadcasted_iota(jnp.int32, (n * rows, 1), 0) // rows
     same_group = row_group == group
-    weights, counts = [], []
+    weights = []
     for index in range(heads):
         scores = lax.dot_general(
             queries[index], keys[:, index * head : (index + 1) * head],
@@ -258,35 +264,33 @@
         ) * (1.0 / math.sqrt(head))
         scores = jnp.where(replaced, -jnp.inf, scores)
         top = jnp.max(scores, axis=-1, keepdims=True)
-        weight = jnp.exp(scores - top).astype(bf16).astype(f32)
+        weight = jnp.exp(scores - top)
         grouped = jnp.where(same_group, jnp.concatenate([weight] * n, axis=0), 0.0)
-        partial = jnp.sum(grouped, axis=-1, keepdims=True).astype(bf16).astype(f32)
-        counts.append(sum(partial[i * rows : (i + 1) * rows] for i in range(n)))
         weights.append(grouped.astype(bf16))
 
     fresh_values = project(2)
     values[stale:, :] = fresh_values
+    ones = jnp.ones((count, head), bf16)
     for index in range(heads):
         span = slice(index * head, (index + 1) * head)
-        partial = jnp.dot(weights[index], values[:, span], preferred_element_type=f32)
+        both = jnp.concatenate([values[:, span], ones], axis=1)
+        partial = jnp.dot(weights[index], both, preferred_element_type=f32)
         partial = partial.astype(bf16).astype(f32)
-        numerator = sum(partial[i * rows : (i + 1) * rows] for i in range(n))
-        att_buf[me, :, span] = (numerator / counts[index]).astype(bf16)
-    for step in range(1, n):
-        send(
-            att_buf.at[me], att_buf.at[me], att_s.at[step], att_r.at[me], {"seq": peer(step)}
-        )
-
-    keys_f32 = keys[stale:, :].astype(f32)
+        sums = sum(partial[i * rows : (i + 1) * rows] for i in range(n))
+        att_buf[me, :, span] = (sums[:, :head] / sums[:, head:]).astype(bf16)
+    for step in range(1, n):
+        send(att_buf.at[me], att_buf.at[me], att_s.at[step], att_r.at[me], {"seq": peer(step)})
+
+    keys_f32 = fresh_keys.astype(f32)
     values_f32 = fresh_values.astype(f32)
+    is_key = lax.broadcasted_iota(jnp.int32, (tokens, 2, cols), 1) == 0
     for index in range(n):
         span = slice(index * tokens, (index + 1) * tokens)
-        which = lax.broadcasted_iota(jnp.int32, (tokens, 2, cols), 1)
         fresh_stage[index] = jnp.where(
-            which == 0, keys_f32[span][:, None, :], values_f32[span][:, None, :]
+            is_key, keys_f32[span][:, None, :], values_f32[span][:, None, :]
         ).astype(bf16)
     own_fresh = pltpu.make_async_copy(
-        fresh_stage.at[me], fresh_hbm.at[0, :, :, cols_of(me)], sem_own.at[2]
+        fresh_stage.at[me], fresh_hbm.at[0, :, :, cols_of(me)], sem_small.at[6]
     )
     own_fresh.start()
     for step in range(1, n):
@@ -294,6 +298,7 @@
             fresh_stage.at[peer(step)], fresh_hbm.at[0, :, :, cols_of(me)],
             fresh_s.at[step], fresh_r.at[me], {"seq": peer(step)},
         )
+    gate = jnp.sum(jnp.where(chosen, mod[2, :, cols_of(me)], 0.0), axis=0, keepdims=True)
 
     for copy in out_copies:
         copy.wait()
@@ -302,10 +307,13 @@
         source = origin(step)
         arrival(att_buf.at[source], att_s.at[step], att_r.at[source], {"seq": source})
         total += jnp.dot(att_buf[source], w_out[source], preferred_element_type=f32)
-    attn_out = total.astype(bf16).astype(f32)
-    block = rows_f32[:, cols_of(me)] + block_gate * attn_out
-    for index in range(n):
-        block_stage[index] = block[index * tokens : (index + 1) * tokens].astype(bf16)
+    for step in range(1, n):
+        source = origin(step)
+        arrival(hid_cols.at[source], hid_s.at[step], hid_r.at[source], {"seq": source})
+    change = gate * total.astype(bf16).astype(f32)
+    for index in range(n):
+        block = hid_cols[index].astype(f32) + change[index * tokens : (index + 1) * tokens]
+        block_stage[index] = block.astype(bf16)
     for index in range(n):
         send(
             block_stage.at[index], next_hbm.at[0, :, cols_of(me)],
@@ -334,12 +342,12 @@
     patches = kv_cache.shape[1]
     cols = w_qkv.shape[3]
     rows = n * tokens
-    stale = n * patches * tokens
+    per = patches * tokens
     chunk = width // 3 if width % 48 == 0 else width
     parts = width // chunk
     bf16, f32 = jnp.bfloat16, jnp.float32
     anywhere = pl.BlockSpec(memory_space=pl.ANY)
-    scalars = pl.BlockSpec(memory_space=pltpu.SMEM)
+    in_hbm = pl.BlockSpec(memory_space=pltpu.HBM)
     dma = pltpu.SemaphoreType.DMA
     return pl.pallas_call(
         functools.partial(fused_kernel, n, sections, chunk),
@@ -347,30 +355,33 @@
             jax.ShapeDtypeStruct(hidden.shape, bf16),
             jax.ShapeDtypeStruct((1, tokens, 2, width), bf16),
         ),
-        in_specs=[scalars] * 2 + [anywhere] * 6,
+        in_specs=[in_hbm] * 8,
         out_specs=(anywhere, anywhere),
         scratch_shapes=[
+            pltpu.VMEM((tokens, width), bf16),
+            pltpu.VMEM((n, tokens, cols), bf16),
             pltpu.VMEM((n, tokens, width), bf16),
             pltpu.VMEM((rows, width), f32),
-            pltpu.VMEM((rows, width), bf16),
-            pltpu.VMEM((n, patches, tokens, 2, cols), bf16),
-            pltpu.VMEM((stale + rows, cols), bf16),
-            pltpu.VMEM((stale + rows, cols), bf16),
+            pltpu.VMEM((patches, tokens, 2, width), bf16),
+            pltpu.VMEM((2, n, per, cols), bf16),
+            pltpu.VMEM((n * per + rows, cols), bf16),
+            pltpu.VMEM((n * per + rows, cols), bf16),
             pltpu.VMEM((3, width, cols), bf16),
             pltpu.VMEM((n, cols, cols), bf16),
             pltpu.VMEM(norm_gain.shape, f32),
             pltpu.VMEM((3, modulation.shape[1], width), f32),
+            pltpu.SMEM(patch_order.shape, jnp.int32),
+            pltpu.SMEM(timestep.shape, jnp.int32),
             pltpu.VMEM((n, tokens, 2, cols), bf16),
             pltpu.VMEM((n, rows, cols), bf16),
             pltpu.VMEM((n, tokens, cols), bf16),
             dma((3, parts)),
             dma((n,)),
-            dma((2,)),
-            dma((3,)),
+            dma((7,)),
         ]
-        + [dma((n,))] * 10,
+        + [dma((n,))] * 14,
         compiler_params=pltpu.CompilerParams(
-            collective_id=0, has_side_effects=True, vmem_limit_bytes=50 * 2**20
+            collective_id=0, has_side_effects=True, vmem_limit_bytes=60 * 2**20
         ),
     )(
         patch_order,
@@ -388,7 +399,8 @@
     hidden, w_qkv, norm_gain = arrays[0], arrays[2], arrays[4]
     lanes = norm_gain.shape[2]
     whole_heads = lanes % 128 == 0 and w_qkv.shape[3] % lanes == 0
-    whole_tiles = lax.axis_size("seq") * hidden.shape[1] % 16 == 0
+    rows, per = lax.axis_size("seq") * hidden.shape[1], arrays[1].shape[1] * hidden.shape[1]
+    whole_tiles = rows % 16 == 0 and per % 16 == 0
     if whole_heads and whole_tiles and lax.axis_size("seq") > 1 and lax.axis_size("section") > 1:
         return fused(*arrays)
     return body(*arrays)

time: 35.3 us -> 28.7 us (0.81)
  Pallas kernels: 28.5 us -> 25 us
  local copies, waits for them, and re-layouts: 5.78 us -> 2.81 us
    pallas_call x1, Pallas kernels: 28.5 us -> 25 us  [fused(): pl.pallas_call(functools.partial(fused_kernel, n, sections, chunk), out_s...]
    unnamed x14 -> x2, local copies, waits for them, and re-layouts: 5.78 us -> 2.81 us
where the time goes in v2:
time: 28.7 us; the launch traced here: 28.5 us
  Pallas kernels  25 us (87%)
  local copies, waits for them, and re-layouts  2.81 us (10%)
  between operations  0.64 us (2%)
    pallas_call x1, Pallas kernels, fused(): pl.pallas_call(functools.partial(fused_kernel, n, sections, chunk), out_s...  25 us
    unnamed x2, local copies, waits for them, and re-layouts  2.81 us

profile of v2, /device:TPU:1, one launch (start us, length us, event | category | flops | bytes accessed | tf_op | source)
XLA Modules:
  0.0 28.5 jit_solution(11265741475012594428)
XLA Ops:
  0.6 25.0 %shard_map.95 = (bf16[1,4,3072]{2,1,0:T(4,128)(2,1)}, bf16[1,4,2,3072]{3,2,1,0:T(2,128)(2,1)}) custom-call(s32[4]{0:T(128)} %patch_hbm.1, s32[4]{0:T(128)} %step_hbm.1, bf16[1,4,3072]{2,1,0:T(4,128)(2,1)} %hidden_hbm.1, bf16[1,4,4,2,3072]{4,3,2,1,0:T(2,128)(2,1)} %cache_hbm.1, bf16[3,3072,768]{2,1,0:T(8,128)(2,1)} %bitcast.7, bf16[4,768,768]{2,1,0:T(8,128)(2,1)} %bitcast.8, ...), custom_call_target="tpu_custom_call" | custom-call | tf_op jit(solution)/shard_map/pallas_call | solution.py:352
  25.7 1.4 %copy.12 = bf16[1,4,3072]{2,1,0:T(4,128)(2,1)} copy(bf16[1,4,3072]{2,1,0:T(4,128)(2,1)} %get-tuple-element.4) | data formatting | bytes 49152
  27.0 1.5 %copy.13 = bf16[1,4,2,3072]{3,2,1,0:T(2,128)(2,1)} copy(bf16[1,4,2,3072]{3,2,1,0:T(2,128)(2,1)} %get-tuple-element.5) | data formatting | bytes 98304

commit v3 on v2

--- a/solution.py
+++ b/solution.py
@@ -116,11 +116,15 @@
     def per_of(index):
         return pl.ds(pl.multiple_of(index * per, per), per)
 
+    upper = me >= n // 2
+    edge = jnp.where(upper, n - 1 - me, me)
+
+    def origin(step):
+        index = step - 1 + jnp.where(edge <= step - 1, 1, 0)
+        return jnp.where(upper, n - 1 - index, index)
+
     def peer(step):
-        return lax.rem(me + step, n)
-
-    def origin(step):
-        return lax.rem(me + n - step, n)
+        return origin(n - step)
 
     barrier = pltpu.get_barrier_semaphore()
     for step in range(1, n):
@@ -147,8 +151,8 @@
     for copy in small:
         copy.start()
     qkv_copies = {}
-    for which in (1, 0, 2):
-        for part in range(parts):
+    for part in range(parts):
+        for which in (1, 0, 2):
             span = pl.ds(part * chunk, chunk)
             copy = pltpu.make_async_copy(
                 qkv_hbm.at[which, span], w_qkv.at[which, span], sem_qkv.at[which, part]
@@ -184,8 +188,10 @@
             device_id=device, device_id_type=MESH,
         ).wait_recv()
 
-    for step in range(1, n):
-        send(norm_buf.at[me], norm_buf.at[me], norm_s.at[step], norm_r.at[me], {"seq": peer(step)})
+    for part in range(parts):
+        piece = norm_buf.at[me, :, pl.ds(part * chunk, chunk)]
+        for step in range(1, n):
+            send(piece, piece, norm_s.at[part, step], norm_r.at[part, me], {"seq": peer(step)})
 
     for copy in small[3:]:
         copy.wait()
@@ -216,20 +222,26 @@
     for copy in out_copies:
         copy.start()
 
-    for step in range(1, n):
-        source = origin(step)
-        arrival(norm_buf.at[source], norm_s.at[step], norm_r.at[source], {"seq": source})
-    for index in range(n):
-        rows_f32[index * tokens : (index + 1) * tokens, :] = norm_buf[index].astype(f32)
-    normed = rows_f32[...].astype(bf16)
-
-    def project(which):
-        total = jnp.zeros((rows, cols), f32)
-        for part in range(parts):
+    totals = [jnp.zeros((rows, cols), f32)] * 3
+    for part in range(parts):
+        span = slice(part * chunk, (part + 1) * chunk)
+        for step in range(1, n):
+            source = origin(step)
+            arrival(
+                norm_buf.at[source, :, pl.ds(part * chunk, chunk)],
+                norm_s.at[part, step], norm_r.at[part, source], {"seq": source},
+            )
+        for index in range(n):
+            rows_f32[index * tokens : (index + 1) * tokens, span] = norm_buf[index, :, span].astype(
+                f32
+            )
+        normed = rows_f32[:, span].astype(bf16)
+        for which in (1, 0, 2):
             qkv_copies[which, part].wait()
-            span = slice(part * chunk, (part + 1) * chunk)
-            total += jnp.dot(normed[:, span], w_qkv[which, span, :], preferred_element_type=f32)
-        return total.astype(bf16)
+            totals[which] += jnp.dot(
+                normed, w_qkv[which, span, :], preferred_element_type=f32
+            )
+    projected = [total.astype(bf16) for total in totals]
 
     def head_norms(projected, which):
         done = []
@@ -240,14 +252,13 @@
             done.append(normal.astype(bf16))
         return done
 
-    fresh_keys = jnp.concatenate(head_norms(project(1), 1), axis=1)
+    fresh_keys = jnp.concatenate(head_norms(projected[1], 1), axis=1)
     keys[stale:, :] = fresh_keys
-    queries = head_norms(project(0), 0)
+    queries = head_norms(projected[0], 0)
 
     for step in range(1, n):
         source = origin(step)
         arrival(keys.at[per_of(source)], key_s.at[step], key_r.at[source], {"seq": source})
-        arrival(values.at[per_of(source)], value_s.at[step], value_r.at[source], {"seq": source})
     count = stale + rows
     column = lax.broadcasted_iota(jnp.int32, (1, count), 1)
     is_cache = column < stale
@@ -268,8 +279,11 @@
         grouped = jnp.where(same_group, jnp.concatenate([weight] * n, axis=0), 0.0)
         weights.append(grouped.astype(bf16))
 
-    fresh_values = project(2)
+    fresh_values = projected[2]
     values[stale:, :] = fresh_values
+    for step in range(1, n):
+        source = origin(step)
+        arrival(values.at[per_of(source)], value_s.at[step], value_r.at[source], {"seq": source})
     ones = jnp.ones((count, head), bf16)
     for index in range(heads):
         span = slice(index * head, (index + 1) * head)
@@ -352,8 +366,8 @@
     return pl.pallas_call(
         functools.partial(fused_kernel, n, sections, chunk),
         out_shape=(
-            jax.ShapeDtypeStruct(hidden.shape, bf16),
-            jax.ShapeDtypeStruct((1, tokens, 2, width), bf16),
+            pltpu.VMEM(hidden.shape, bf16),
+            pltpu.VMEM((1, tokens, 2, width), bf16),
         ),
         in_specs=[in_hbm] * 8,
         out_specs=(anywhere, anywhere),
@@ -378,8 +392,10 @@
             dma((3, parts)),
             dma((n,)),
             dma((7,)),
+            dma((parts, n)),
+            dma((parts, n)),
         ]
-        + [dma((n,))] * 14,
+        + [dma((n,))] * 12,
         compiler_params=pltpu.CompilerParams(
             collective_id=0, has_side_effects=True, vmem_limit_bytes=60 * 2**20
         ),

time: 28.7 us -> 24.8 us (0.86)
  Pallas kernels: 25 us -> 22.8 us
  local copies, waits for them, and re-layouts: 2.81 us -> 1.23 us
    pallas_call x1, Pallas kernels: 25 us -> 22.8 us  [fused(): pl.pallas_call(functools.partial(fused_kernel, n, sections, chunk), out_s...]
    unnamed x2, local copies, waits for them, and re-layouts: 2.81 us -> 1.23 us
where the time goes in v3:
time: 24.8 us; the launch traced here: 24.7 us
  Pallas kernels  22.8 us (92%)
  local copies, waits for them, and re-layouts  1.23 us (5%)
  between operations  0.64 us (3%)
    pallas_call x1, Pallas kernels, fused(): pl.pallas_call(functools.partial(fused_kernel, n, sections, chunk), out_s...  22.8 us
    unnamed x2, local copies, waits for them, and re-layouts  1.23 us

profile of v3, /device:TPU:1, one launch (start us, length us, event | category | flops | bytes accessed | tf_op | source)
XLA Modules:
  0.0 24.7 jit_solution(18219308328326049243)
XLA Ops:
  0.6 22.8 %shard_map.95 = (bf16[1,4,3072]{2,1,0:T(4,128)(2,1)S(1)}, bf16[1,4,2,3072]{3,2,1,0:T(2,128)(2,1)S(1)}) custom-call(s32[4]{0:T(128)} %patch_hbm.1, s32[4]{0:T(128)} %step_hbm.1, bf16[1,4,3072]{2,1,0:T(4,128)(2,1)} %hidden_hbm.1, bf16[1,4,4,2,3072]{4,3,2,1,0:T(2,128)(2,1)} %cache_hbm.1, bf16[3,3072,768]{2,1,0:T(8,128)(2,1)} %bitcast.7, ...), custom_call_target="tpu_custom_call" | custom-call | tf_op jit(solution)/shard_map/pallas_call | solution.py:366
  23.4 0.6 %copy.12 = bf16[1,4,3072]{2,1,0:T(4,128)(2,1)} copy(bf16[1,4,3072]{2,1,0:T(4,128)(2,1)S(1)} %get-tuple-element.2) | data formatting | bytes 49152
  24.1 0.6 %copy.13 = bf16[1,4,2,3072]{3,2,1,0:T(2,128)(2,1)} copy(bf16[1,4,2,3072]{3,2,1,0:T(2,128)(2,1)S(1)} %get-tuple-element.3) | data formatting | bytes 98304

commit v4 on v3

--- a/solution.py
+++ b/solution.py
@@ -90,7 +90,7 @@
     n, sections, chunk,
     patch_hbm, step_hbm, hidden_hbm, cache_hbm, qkv_hbm, out_hbm, gain_hbm, mod_hbm,
     next_hbm, fresh_hbm,
-    own_rows, hid_cols, norm_buf, rows_f32, own_cache, cache_stage, keys, values, w_qkv, w_out,
+    own_rows, hid_cols, norm_buf, rows_f32, own_cache, cache_stage, cache_in, all_f32, w_qkv, w_out,
     gain, mod, patch, step_at, fresh_stage, att_buf, block_stage,
     sem_qkv, sem_out, sem_small, norm_s, norm_r, hid_s, hid_r, key_s, key_r, value_s, value_r,
     fresh_s, fresh_r, att_s, att_r, blk_s, blk_r,
@@ -106,15 +106,13 @@
     head = gain.shape[2]
     heads = cols // head
     rows = n * tokens
-    per = patches * tokens
+    kept = patches - 1
+    per = kept * tokens
     stale = n * per
     parts = width // chunk
 
     def cols_of(index):
         return pl.ds(pl.multiple_of(index * cols, head), cols)
-
-    def per_of(index):
-        return pl.ds(pl.multiple_of(index * per, per), per)
 
     upper = me >= n // 2
     edge = jnp.where(upper, n - 1 - me, me)
@@ -195,20 +193,20 @@
 
     for copy in small[3:]:
         copy.wait()
-    pair = own_cache[...].astype(f32).reshape(per, 2, width)
-    for which in range(2):
-        split = pair[:, which, :].astype(bf16)
-        for index in range(n):
-            cache_stage[which, index] = split[:, index * cols : (index + 1) * cols]
-    for which, (into, send_sem, recv_sem) in enumerate(
-        ((keys, key_s, key_r), (values, value_s, value_r))
-    ):
+    held = patch[section]
+    for slot in range(kept):
+        pair = jnp.where(held <= slot, own_cache[slot + 1], own_cache[slot]).astype(f32)
+        for which in range(2):
+            split = pair[:, which, :].astype(bf16)
+            for index in range(n):
+                cache_stage[which, index, slot] = split[:, index * cols : (index + 1) * cols]
+    for which, (send_sem, recv_sem) in enumerate(((key_s, key_r), (value_s, value_r))):
         for step in range(1, n):
             send(
-                cache_stage.at[which, peer(step)], into.at[per_of(me)],
+                cache_stage.at[which, peer(step)], cache_in.at[which, me],
                 send_sem.at[step], recv_sem.at[me], {"seq": peer(step)},
             )
-        into[per_of(me), :] = cache_stage[which, me]
+        cache_in[which, me] = cache_stage[which, me]
     for step in range(1, n):
         send(
             own_rows.at[:, cols_of(peer(step))], hid_cols.at[me], hid_s.at[step], hid_r.at[me],
@@ -252,19 +250,25 @@
             done.append(normal.astype(bf16))
         return done
 
+    def gathered(which, fresh, send_sem, recv_sem):
+        for step in range(1, n):
+            source = origin(step)
+            arrival(
+                cache_in.at[which, source], send_sem.at[step], recv_sem.at[source], {"seq": source}
+            )
+        for index in range(n):
+            for slot in range(kept):
+                first = index * per + slot * tokens
+                all_f32[which, first : first + tokens, :] = cache_in[which, index, slot].astype(f32)
+        all_f32[which, stale:, :] = fresh.astype(f32)
+        return all_f32[which].astype(bf16)
+
     fresh_keys = jnp.concatenate(head_norms(projected[1], 1), axis=1)
-    keys[stale:, :] = fresh_keys
     queries = head_norms(projected[0], 0)
-
-    for step in range(1, n):
-        source = origin(step)
-        arrival(keys.at[per_of(source)], key_s.at[step], key_r.at[source], {"seq": source})
+    keys = gathered(0, fresh_keys, key_s, key_r)
     count = stale + rows
     column = lax.broadcasted_iota(jnp.int32, (1, count), 1)
-    is_cache = column < stale
-    in_patch = lax.rem(column // tokens, patches)
-    replaced = jnp.logical_and(is_cache, in_patch == patch[section])
-    group = jnp.where(is_cache, column // per, (column - stale) // tokens)
+    group = jnp.where(column < stale, column // per, (column - stale) // tokens)
     row_group = lax.broadcasted_iota(jnp.int32, (n * rows, 1), 0) // rows
     same_group = row_group == group
     weights = []
@@ -273,17 +277,13 @@
             queries[index], keys[:, index * head : (index + 1) * head],
             (((1,), (1,)), ((), ())), preferred_element_type=f32,
         ) * (1.0 / math.sqrt(head))
-        scores = jnp.where(replaced, -jnp.inf, scores)
         top = jnp.max(scores, axis=-1, keepdims=True)
         weight = jnp.exp(scores - top)
         grouped = jnp.where(same_group, jnp.concatenate([weight] * n, axis=0), 0.0)
         weights.append(grouped.astype(bf16))
 
     fresh_values = projected[2]
-    values[stale:, :] = fresh_values
-    for step in range(1, n):
-        source = origin(step)
-        arrival(values.at[per_of(source)], value_s.at[step], value_r.at[source], {"seq": source})
+    values = gathered(1, fresh_values, value_s, value_r)
     ones = jnp.ones((count, head), bf16)
     for index in range(heads):
         span = slice(index * head, (index + 1) * head)
@@ -349,6 +349,17 @@
         copy.wait_send()
 
 
+def place_kernel(next_ref, fresh_ref, next_out, fresh_out, sems):
+    copies = [
+        pltpu.make_async_copy(next_ref, next_out, sems.at[0]),
+        pltpu.make_async_copy(fresh_ref, fresh_out, sems.at[1]),
+    ]
+    for copy in copies:
+        copy.start()
+    for copy in copies:
+        copy.wait()
+
+
 def fused(hidden, kv_cache, w_qkv, w_out, norm_gain, modulation, patch_order, timestep):
     n = lax.axis_size("seq")
     sections = lax.axis_size("section")
@@ -356,14 +367,13 @@
     patches = kv_cache.shape[1]
     cols = w_qkv.shape[3]
     rows = n * tokens
-    per = patches * tokens
     chunk = width // 3 if width % 48 == 0 else width
     parts = width // chunk
     bf16, f32 = jnp.bfloat16, jnp.float32
     anywhere = pl.BlockSpec(memory_space=pl.ANY)
     in_hbm = pl.BlockSpec(memory_space=pltpu.HBM)
     dma = pltpu.SemaphoreType.DMA
-    return pl.pallas_call(
+    results = pl.pallas_call(
         functools.partial(fused_kernel, n, sections, chunk),
         out_shape=(
             pltpu.VMEM(hidden.shape, bf16),
@@ -377,9 +387,9 @@
             pltpu.VMEM((n, tokens, width), bf16),
             pltpu.VMEM((rows, width), f32),
             pltpu.VMEM((patches, tokens, 2, width), bf16),
-            pltpu.VMEM((2, n, per, cols), bf16),
-            pltpu.VMEM((n * per + rows, cols), bf16),
-            pltpu.VMEM((n * per + rows, cols), bf16),
+            pltpu.VMEM((2, n, patches - 1, tokens, cols), bf16),
+            pltpu.VMEM((2, n, patches - 1, tokens, cols), bf16),
+            pltpu.VMEM((2, patches * rows, cols), f32),
             pltpu.VMEM((3, width, cols), bf16),
             pltpu.VMEM((n, cols, cols), bf16),
             pltpu.VMEM(norm_gain.shape, f32),
@@ -409,14 +419,20 @@
         norm_gain,
         jnp.transpose(modulation[0], (1, 0, 2)),
     )
+    return pl.pallas_call(
+        place_kernel,
+        out_shape=tuple(jax.ShapeDtypeStruct(result.shape, bf16) for result in results),
+        in_specs=[anywhere] * 2,
+        out_specs=(anywhere, anywhere),
+        scratch_shapes=[dma((2,))],
+    )(*results)
 
 
 def block_step(*arrays):
     hidden, w_qkv, norm_gain = arrays[0], arrays[2], arrays[4]
     lanes = norm_gain.shape[2]
     whole_heads = lanes % 128 == 0 and w_qkv.shape[3] % lanes == 0
-    rows, per = lax.axis_size("seq") * hidden.shape[1], arrays[1].shape[1] * hidden.shape[1]
-    whole_tiles = rows % 16 == 0 and per % 16 == 0
+    whole_tiles = lax.axis_size("seq") * hidden.shape[1] % 16 == 0 and arrays[1].shape[1] > 1
     if whole_heads and whole_tiles and lax.axis_size("seq") > 1 and lax.axis_size("section") > 1:
         return fused(*arrays)
     return body(*arrays)

time: 24.8 us -> 27.4 us (1.10)
  Pallas kernels: 22.8 us -> 25.4 us
    pallas_call x0 -> x1, Pallas kernels: none -> 3.35 us  [fused(): pl.pallas_call(place_kernel, out_shape=tuple((jax.ShapeDtypeStruct(result...]
    pallas_call x1, Pallas kernels: 22.8 us -> 22 us  [fused(): pl.pallas_call(functools.partial(fused_kernel, n, sections, chunk), out_s...]
    unnamed x2 -> x4, local copies, waits for them, and re-layouts: 1.23 us -> 1.21 us
where the time goes in v4:
time: 27.4 us; the launch traced here: 27.2 us
  Pallas kernels  25.4 us (93%)
  local copies, waits for them, and re-layouts  1.21 us (4%)
  between operations  0.65 us (2%)
    pallas_call x1, Pallas kernels, fused(): pl.pallas_call(functools.partial(fused_kernel, n, sections, chunk), out_s...  22 us
    pallas_call x1, Pallas kernels, fused(): pl.pallas_call(place_kernel, out_shape=tuple((jax.ShapeDtypeStruct(result...  3.35 us
    unnamed x4, local copies, waits for them, and re-layouts  1.21 us

profile of v4, /device:TPU:1, one launch (start us, length us, event | category | flops | bytes accessed | tf_op | source)
XLA Modules:
  0.0 27.2 jit_solution(14603277283951444506)
XLA Ops:
  0.6 22.0 %shard_map.95 = (bf16[1,4,3072]{2,1,0:T(4,128)(2,1)S(1)}, bf16[1,4,2,3072]{3,2,1,0:T(2,128)(2,1)S(1)}) custom-call(s32[4]{0:T(128)} %patch_hbm.1, s32[4]{0:T(128)} %step_hbm.1, bf16[1,4,3072]{2,1,0:T(4,128)(2,1)} %hidden_hbm.1, bf16[1,4,4,2,3072]{4,3,2,1,0:T(2,128)(2,1)} %cache_hbm.1, bf16[3,3072,768]{2,1,0:T(8,128)(2,1)} %bitcast.7, ...), custom_call_target="tpu_custom_call" | custom-call | tf_op jit(solution)/shard_map/pallas_call | solution.py:376
  22.7 0.0 copy-start
  22.7 0.6 %copy-done = bf16[1,4,2,3072]{3,2,1,0:T(2,128)(2,1)} copy-done((bf16[1,4,2,3072]{3,2,1,0:T(2,128)(2,1)}, bf16[1,4,2,3072]{3,2,1,0:T(2,128)(2,1)S(1)}, u32[]{:S(2)}) %copy-start) | copy-done | bytes 49176
  23.3 0.0 copy-start.1
  23.3 0.6 %copy-done.1 = bf16[1,4,3072]{2,1,0:T(4,128)(2,1)} copy-done((bf16[1,4,3072]{2,1,0:T(4,128)(2,1)}, bf16[1,4,3072]{2,1,0:T(4,128)(2,1)S(1)}, u32[]{:S(2)}) %copy-start.1) | copy-done | bytes 24600
  23.9 3.4 %shard_map.96 = (bf16[1,4,3072]{2,1,0:T(4,128)(2,1)}, bf16[1,4,2,3072]{3,2,1,0:T(2,128)(2,1)}) custom-call(bf16[1,4,3072]{2,1,0:T(4,128)(2,1)} %copy-done.1, bf16[1,4,2,3072]{3,2,1,0:T(2,128)(2,1)} %copy-done), custom_call_target="tpu_custom_call" | custom-call | tf_op jit(solution)/shard_map/pallas_call | solution.py:422
Async XLA Ops:
  22.7 0.6 %copy-start = (bf16[1,4,2,3072]{3,2,1,0:T(2,128)(2,1)}, bf16[1,4,2,3072]{3,2,1,0:T(2,128)(2,1)S(1)}, u32[]{:S(2)}) copy-start(bf16[1,4,2,3072]{3,2,1,0:T(2,128)(2,1)S(1)} %get-tuple-element.5.fresh_ref) | copy-start | bytes 147460
  23.3 0.6 %copy-start.1 = (bf16[1,4,3072]{2,1,0:T(4,128)(2,1)}, bf16[1,4,3072]{2,1,0:T(4,128)(2,1)S(1)}, u32[]{:S(2)}) copy-start(bf16[1,4,3072]{2,1,0:T(4,128)(2,1)S(1)} %get-tuple-element.4.next_ref) | copy-start | bytes 73732

commit v5 on v4

--- a/solution.py
+++ b/solution.py
@@ -155,8 +155,9 @@
             copy = pltpu.make_async_copy(
                 qkv_hbm.at[which, span], w_qkv.at[which, span], sem_qkv.at[which, part]
             )
-            copy.start()
             qkv_copies[which, part] = copy
+            if part == 0:
+                copy.start()
 
     for copy in small[:3]:
         copy.wait()
@@ -190,6 +191,10 @@
         piece = norm_buf.at[me, :, pl.ds(part * chunk, chunk)]
         for step in range(1, n):
             send(piece, piece, norm_s.at[part, step], norm_r.at[part, me], {"seq": peer(step)})
+
+    for (which, part), copy in qkv_copies.items():
+        if part > 0:
+            copy.start()
 
     for copy in small[3:]:
         copy.wait()
@@ -283,18 +288,6 @@
         weights.append(grouped.astype(bf16))
 
     fresh_values = projected[2]
-    values = gathered(1, fresh_values, value_s, value_r)
-    ones = jnp.ones((count, head), bf16)
-    for index in range(heads):
-        span = slice(index * head, (index + 1) * head)
-        both = jnp.concatenate([values[:, span], ones], axis=1)
-        partial = jnp.dot(weights[index], both, preferred_element_type=f32)
-        partial = partial.astype(bf16).astype(f32)
-        sums = sum(partial[i * rows : (i + 1) * rows] for i in range(n))
-        att_buf[me, :, span] = (sums[:, :head] / sums[:, head:]).astype(bf16)
-    for step in range(1, n):
-        send(att_buf.at[me], att_buf.at[me], att_s.at[step], att_r.at[me], {"seq": peer(step)})
-
     keys_f32 = fresh_keys.astype(f32)
     values_f32 = fresh_values.astype(f32)
     is_key = lax.broadcasted_iota(jnp.int32, (tokens, 2, cols), 1) == 0
@@ -312,6 +305,18 @@
             fresh_stage.at[peer(step)], fresh_hbm.at[0, :, :, cols_of(me)],
             fresh_s.at[step], fresh_r.at[me], {"seq": peer(step)},
         )
+    values = gathered(1, fresh_values, value_s, value_r)
+    ones = jnp.ones((count, head), bf16)
+    for index in range(heads):
+        span = slice(index * head, (index + 1) * head)
+        both = jnp.concatenate([values[:, span], ones], axis=1)
+        partial = jnp.dot(weights[index], both, preferred_element_type=f32)
+        partial = partial.astype(bf16).astype(f32)
+        sums = sum(partial[i * rows : (i + 1) * rows] for i in range(n))
+        att_buf[me, :, span] = (sums[:, :head] / sums[:, head:]).astype(bf16)
+    for step in range(1, n):
+        send(att_buf.at[me], att_buf.at[me], att_s.at[step], att_r.at[me], {"seq": peer(step)})
+
     gate = jnp.sum(jnp.where(chosen, mod[2, :, cols_of(me)], 0.0), axis=0, keepdims=True)
 
     for copy in out_copies:
@@ -347,17 +352,6 @@
         )
     for copy in sends:
         copy.wait_send()
-
-
-def place_kernel(next_ref, fresh_ref, next_out, fresh_out, sems):
-    copies = [
-        pltpu.make_async_copy(next_ref, next_out, sems.at[0]),
-        pltpu.make_async_copy(fresh_ref, fresh_out, sems.at[1]),
-    ]
-    for copy in copies:
-        copy.start()
-    for copy in copies:
-        copy.wait()
 
 
 def fused(hidden, kv_cache, w_qkv, w_out, norm_gain, modulation, patch_order, timestep):
@@ -373,7 +367,7 @@
     anywhere = pl.BlockSpec(memory_space=pl.ANY)
     in_hbm = pl.BlockSpec(memory_space=pltpu.HBM)
     dma = pltpu.SemaphoreType.DMA
-    results = pl.pallas_call(
+    return pl.pallas_call(
         functools.partial(fused_kernel, n, sections, chunk),
         out_shape=(
             pltpu.VMEM(hidden.shape, bf16),
@@ -419,13 +413,6 @@
         norm_gain,
         jnp.transpose(modulation[0], (1, 0, 2)),
     )
-    return pl.pallas_call(
-        place_kernel,
-        out_shape=tuple(jax.ShapeDtypeStruct(result.shape, bf16) for result in results),
-        in_specs=[anywhere] * 2,
-        out_specs=(anywhere, anywhere),
-        scratch_shapes=[dma((2,))],
-    )(*results)
 
 
 def block_step(*arrays):

time: 27.4 us -> 23.9 us (0.87)
  Pallas kernels: 25.4 us -> 21.9 us
    pallas_call x1 -> x0, Pallas kernels: 3.35 us -> none  [fused(): pl.pallas_call(place_kernel, out_shape=tuple((jax.ShapeDtypeStruct(result...]
    unnamed x4 -> x2, local copies, waits for them, and re-layouts: 1.21 us -> 1.23 us
where the time goes in v5:
time: 23.9 us; the launch traced here: 23.8 us
  Pallas kernels  21.9 us (92%)
  local copies, waits for them, and re-layouts  1.23 us (5%)
  between operations  0.64 us (3%)
    pallas_call x1, Pallas kernels, fused(): pl.pallas_call(functools.partial(fused_kernel, n, sections, chunk), out_s...  21.9 us
    unnamed x2, local copies, waits for them, and re-layouts  1.23 us

profile of v5, /device:TPU:1, one launch (start us, length us, event | category | flops | bytes accessed | tf_op | source)
XLA Modules:
  0.0 23.8 jit_solution(12862662462123782605)
XLA Ops:
  0.6 21.9 %shard_map.95 = (bf16[1,4,3072]{2,1,0:T(4,128)(2,1)S(1)}, bf16[1,4,2,3072]{3,2,1,0:T(2,128)(2,1)S(1)}) custom-call(s32[4]{0:T(128)} %patch_hbm.1, s32[4]{0:T(128)} %step_hbm.1, bf16[1,4,3072]{2,1,0:T(4,128)(2,1)} %hidden_hbm.1, bf16[1,4,4,2,3072]{4,3,2,1,0:T(2,128)(2,1)} %cache_hbm.1, bf16[3,3072,768]{2,1,0:T(8,128)(2,1)} %bitcast.7, ...), custom_call_target="tpu_custom_call" | custom-call | tf_op jit(solution)/shard_map/pallas_call | solution.py:370
  22.5 0.6 %copy.12 = bf16[1,4,3072]{2,1,0:T(4,128)(2,1)} copy(bf16[1,4,3072]{2,1,0:T(4,128)(2,1)S(1)} %get-tuple-element.2) | data formatting | bytes 49152
  23.2 0.6 %copy.13 = bf16[1,4,2,3072]{3,2,1,0:T(2,128)(2,1)} copy(bf16[1,4,2,3072]{3,2,1,0:T(2,128)(2,1)S(1)} %get-tuple-element.3) | data formatting | bytes 98304

commit v6 on v5

--- a/solution.py
+++ b/solution.py
@@ -87,7 +87,7 @@
 
 
 def fused_kernel(
-    n, sections, chunk,
+    n, sections, chunk, cuts,
     patch_hbm, step_hbm, hidden_hbm, cache_hbm, qkv_hbm, out_hbm, gain_hbm, mod_hbm,
     next_hbm, fresh_hbm,
     own_rows, hid_cols, norm_buf, rows_f32, own_cache, cache_stage, cache_in, all_f32, w_qkv, w_out,
@@ -225,7 +225,7 @@
     for copy in out_copies:
         copy.start()
 
-    totals = [jnp.zeros((rows, cols), f32)] * 3
+    totals = [jnp.zeros((rows, cuts[0][1]), f32)] * 3
     for part in range(parts):
         span = slice(part * chunk, (part + 1) * chunk)
         for step in range(1, n):
@@ -242,59 +242,75 @@
         for which in (1, 0, 2):
             qkv_copies[which, part].wait()
             totals[which] += jnp.dot(
-                normed, w_qkv[which, span, :], preferred_element_type=f32
-            )
-    projected = [total.astype(bf16) for total in totals]
+                normed, w_qkv[which, span, : cuts[0][1]], preferred_element_type=f32
+            )
+    normed = rows_f32[...].astype(bf16)
+    projected = [[total.astype(bf16) for total in totals]]
+
+    def arrivals(which, send_sem, recv_sem):
+        for step in range(1, n):
+            source = origin(step)
+            arrival(
+                cache_in.at[which, source], send_sem.at[step], recv_sem.at[source], {"seq": source}
+            )
+        for index in range(n):
+            for slot in range(kept):
+                first = index * per + slot * tokens
+                all_f32[which, first : first + tokens, :] = cache_in[which, index, slot].astype(f32)
 
     def head_norms(projected, which):
         done = []
-        for index in range(heads):
+        for index in range(projected.shape[1] // head):
             vector = projected[:, index * head : (index + 1) * head].astype(f32)
             square = jnp.mean(vector * vector, axis=-1, keepdims=True)
             normal = vector * lax.rsqrt(square + 1e-06) * gain[0, which : which + 1, :]
             done.append(normal.astype(bf16))
         return done
 
-    def gathered(which, fresh, send_sem, recv_sem):
-        for step in range(1, n):
-            source = origin(step)
-            arrival(
-                cache_in.at[which, source], send_sem.at[step], recv_sem.at[source], {"seq": source}
-            )
-        for index in range(n):
-            for slot in range(kept):
-                first = index * per + slot * tokens
-                all_f32[which, first : first + tokens, :] = cache_in[which, index, slot].astype(f32)
-        all_f32[which, stale:, :] = fresh.astype(f32)
-        return all_f32[which].astype(bf16)
-
-    fresh_keys = jnp.concatenate(head_norms(projected[1], 1), axis=1)
-    queries = head_norms(projected[0], 0)
-    keys = gathered(0, fresh_keys, key_s, key_r)
     count = stale + rows
     column = lax.broadcasted_iota(jnp.int32, (1, count), 1)
     group = jnp.where(column < stale, column // per, (column - stale) // tokens)
     row_group = lax.broadcasted_iota(jnp.int32, (n * rows, 1), 0) // rows
     same_group = row_group == group
-    weights = []
-    for index in range(heads):
-        scores = lax.dot_general(
-            queries[index], keys[:, index * head : (index + 1) * head],
-            (((1,), (1,)), ((), ())), preferred_element_type=f32,
-        ) * (1.0 / math.sqrt(head))
-        top = jnp.max(scores, axis=-1, keepdims=True)
-        weight = jnp.exp(scores - top)
-        grouped = jnp.where(same_group, jnp.concatenate([weight] * n, axis=0), 0.0)
-        weights.append(grouped.astype(bf16))
-
-    fresh_values = projected[2]
-    keys_f32 = fresh_keys.astype(f32)
-    values_f32 = fresh_values.astype(f32)
+    ones = jnp.ones((count, head), bf16)
+
+    def prepare(projected, first):
+        fresh = jnp.concatenate(head_norms(projected[1], 1), axis=1)
+        span = slice(first, first + fresh.shape[1])
+        all_f32[0, stale:, span] = fresh.astype(f32)
+        all_f32[1, stale:, span] = projected[2].astype(f32)
+        return head_norms(projected[0], 0)
+
+    def weigh(queries, first):
+        weights = []
+        for index, query in enumerate(queries):
+            span = slice(first + index * head, first + (index + 1) * head)
+            scores = lax.dot_general(
+                query, all_f32[0, :, span].astype(bf16),
+                (((1,), (1,)), ((), ())), preferred_element_type=f32,
+            ) * (1.0 / math.sqrt(head))
+            top = jnp.max(scores, axis=-1, keepdims=True)
+            weight = jnp.exp(scores - top)
+            grouped = jnp.where(same_group, jnp.concatenate([weight] * n, axis=0), 0.0)
+            weights.append(grouped.astype(bf16))
+        return weights
+
+    arrivals(0, key_s, key_r)
+    for first, last in cuts[1:]:
+        projected.append(
+            [
+                jnp.dot(normed, w_qkv[which, :, first:last], preferred_element_type=f32).astype(bf16)
+                for which in range(3)
+            ]
+        )
+    queries = [prepare(part, first) for (first, _), part in zip(cuts, projected)]
+    weights = weigh(queries[0], 0)
+
     is_key = lax.broadcasted_iota(jnp.int32, (tokens, 2, cols), 1) == 0
     for index in range(n):
-        span = slice(index * tokens, (index + 1) * tokens)
+        span = slice(stale + index * tokens, stale + (index + 1) * tokens)
         fresh_stage[index] = jnp.where(
-            is_key, keys_f32[span][:, None, :], values_f32[span][:, None, :]
+            is_key, all_f32[0, span, :][:, None, :], all_f32[1, span, :][:, None, :]
         ).astype(bf16)
     own_fresh = pltpu.make_async_copy(
         fresh_stage.at[me], fresh_hbm.at[0, :, :, cols_of(me)], sem_small.at[6]
@@ -305,27 +321,37 @@
             fresh_stage.at[peer(step)], fresh_hbm.at[0, :, :, cols_of(me)],
             fresh_s.at[step], fresh_r.at[me], {"seq": peer(step)},
         )
-    values = gathered(1, fresh_values, value_s, value_r)
-    ones = jnp.ones((count, head), bf16)
-    for index in range(heads):
-        span = slice(index * head, (index + 1) * head)
-        both = jnp.concatenate([values[:, span], ones], axis=1)
-        partial = jnp.dot(weights[index], both, preferred_element_type=f32)
-        partial = partial.astype(bf16).astype(f32)
-        sums = sum(partial[i * rows : (i + 1) * rows] for i in range(n))
-        att_buf[me, :, span] = (sums[:, :head] / sums[:, head:]).astype(bf16)
-    for step in range(1, n):
-        send(att_buf.at[me], att_buf.at[me], att_s.at[step], att_r.at[me], {"seq": peer(step)})
+    arrivals(1, value_s, value_r)
+    for place, (first, last) in enumerate(cuts):
+        if place > 0:
+            weights += weigh(queries[place], first)
+        for index in range(first // head, last // head):
+            span = slice(index * head, (index + 1) * head)
+            both = jnp.concatenate([all_f32[1, :, span].astype(bf16), ones], axis=1)
+            partial = jnp.dot(weights[index], both, preferred_element_type=f32)
+            partial = partial.astype(bf16).astype(f32)
+            sums = sum(partial[i * rows : (i + 1) * rows] for i in range(n))
+            att_buf[me, :, span] = (sums[:, :head] / sums[:, head:]).astype(bf16)
+        piece = att_buf.at[me, :, pl.ds(first, last - first)]
+        for step in range(1, n):
+            send(piece, piece, att_s.at[place, step], att_r.at[place, me], {"seq": peer(step)})
 
     gate = jnp.sum(jnp.where(chosen, mod[2, :, cols_of(me)], 0.0), axis=0, keepdims=True)
 
     for copy in out_copies:
         copy.wait()
     total = jnp.dot(att_buf[me], w_out[me], preferred_element_type=f32)
-    for step in range(1, n):
-        source = origin(step)
-        arrival(att_buf.at[source], att_s.at[step], att_r.at[source], {"seq": source})
-        total += jnp.dot(att_buf[source], w_out[source], preferred_element_type=f32)
+    for place, (first, last) in enumerate(cuts):
+        for step in range(1, n):
+            source = origin(step)
+            arrival(
+                att_buf.at[source, :, pl.ds(first, last - first)],
+                att_s.at[place, step], att_r.at[place, source], {"seq": source},
+            )
+            total += jnp.dot(
+                att_buf[source, :, first:last], w_out[source, first:last, :],
+                preferred_element_type=f32,
+            )
     for step in range(1, n):
         source = origin(step)
         arrival(hid_cols.at[source], hid_s.at[step], hid_r.at[source], {"seq": source})
@@ -363,12 +389,16 @@
     rows = n * tokens
     chunk = width // 3 if width % 48 == 0 else width
     parts = width // chunk
+    wide = cols * 2 // 3 // 256 * 256
+    if wide % norm_gain.shape[2]:
+        wide = 0
+    cuts = ((0, wide), (wide, cols)) if wide else ((0, cols),)
     bf16, f32 = jnp.bfloat16, jnp.float32
     anywhere = pl.BlockSpec(memory_space=pl.ANY)
     in_hbm = pl.BlockSpec(memory_space=pltpu.HBM)
     dma = pltpu.SemaphoreType.DMA
     return pl.pallas_call(
-        functools.partial(fused_kernel, n, sections, chunk),
+        functools.partial(fused_kernel, n, sections, chunk, cuts),
         out_shape=(
             pltpu.VMEM(hidden.shape, bf16),
             pltpu.VMEM((1, tokens, 2, width), bf16),
@@ -399,7 +429,9 @@
             dma((parts, n)),
             dma((parts, n)),
         ]
-        + [dma((n,))] * 12,
+        + [dma((n,))] * 8
+        + [dma((len(cuts), n))] * 2
+        + [dma((n,))] * 2,
         compiler_params=pltpu.CompilerParams(
             collective_id=0, has_side_effects=True, vmem_limit_bytes=60 * 2**20
         ),

time: 23.9 us -> 24.1 us (level)
  no operation moved by 1% of the time
where the time goes in v6:
time: 24.1 us; the launch traced here: 23.9 us
  Pallas kernels  22.1 us (92%)
  local copies, waits for them, and re-layouts  1.23 us (5%)
  between operations  0.64 us (3%)
    pallas_call x1, Pallas kernels, fused(): pl.pallas_call(functools.partial(fused_kernel, n, sections, chunk, cuts),...  22.1 us
    unnamed x2, local copies, waits for them, and re-layouts  1.23 us

profile of v6, /device:TPU:1, one launch (start us, length us, event | category | flops | bytes accessed | tf_op | source)
XLA Modules:
  0.0 23.9 jit_solution(11086958514684420302)
XLA Ops:
  0.6 22.1 %shard_map.95 = (bf16[1,4,3072]{2,1,0:T(4,128)(2,1)S(1)}, bf16[1,4,2,3072]{3,2,1,0:T(2,128)(2,1)S(1)}) custom-call(s32[4]{0:T(128)} %patch_hbm.1, s32[4]{0:T(128)} %step_hbm.1, bf16[1,4,3072]{2,1,0:T(4,128)(2,1)} %hidden_hbm.1, bf16[1,4,4,2,3072]{4,3,2,1,0:T(2,128)(2,1)} %cache_hbm.1, bf16[3,3072,768]{2,1,0:T(8,128)(2,1)} %bitcast.7, ...), custom_call_target="tpu_custom_call" | custom-call | tf_op jit(solution)/shard_map/pallas_call | solution.py:400
  22.7 0.6 %copy.12 = bf16[1,4,3072]{2,1,0:T(4,128)(2,1)} copy(bf16[1,4,3072]{2,1,0:T(4,128)(2,1)S(1)} %get-tuple-element.2) | data formatting | bytes 49152
  23.3 0.6 %copy.13 = bf16[1,4,2,3072]{3,2,1,0:T(2,128)(2,1)} copy(bf16[1,4,2,3072]{3,2,1,0:T(2,128)(2,1)S(1)} %get-tuple-element.3) | data formatting | bytes 98304

commit v7 on v6

--- a/solution.py
+++ b/solution.py
@@ -89,10 +89,10 @@
 def fused_kernel(
     n, sections, chunk, cuts,
     patch_hbm, step_hbm, hidden_hbm, cache_hbm, qkv_hbm, out_hbm, gain_hbm, mod_hbm,
-    next_hbm, fresh_hbm,
-    own_rows, hid_cols, norm_buf, rows_f32, own_cache, cache_stage, cache_in, all_f32, w_qkv, w_out,
+    next_ref, fresh_hbm,
+    own_rows, prev_rows, gate_row, prev_gate, landed, norm_buf, rows_f32, own_cache, cache_stage, cache_in, all_f32, w_qkv, w_out,
     gain, mod, patch, step_at, fresh_stage, att_buf, block_stage,
-    sem_qkv, sem_out, sem_small, norm_s, norm_r, hid_s, hid_r, key_s, key_r, value_s, value_r,
+    sem_qkv, sem_out, sem_small, norm_s, norm_r, hid_sems, key_s, key_r, value_s, value_r,
     fresh_s, fresh_r, att_s, att_r, blk_s, blk_r,
 ):
     f32, bf16 = jnp.float32, jnp.bfloat16
@@ -212,12 +212,9 @@
                 send_sem.at[step], recv_sem.at[me], {"seq": peer(step)},
             )
         cache_in[which, me] = cache_stage[which, me]
-    for step in range(1, n):
-        send(
-            own_rows.at[:, cols_of(peer(step))], hid_cols.at[me], hid_s.at[step], hid_r.at[me],
-            {"seq": peer(step)},
-        )
-    hid_cols[me] = own_rows[:, cols_of(me)]
+    gate_row[...] = jnp.sum(jnp.where(chosen, mod[2], 0.0), axis=0, keepdims=True)
+    send(own_rows, prev_rows, hid_sems.at[0], hid_sems.at[1], {"section": after})
+    send(gate_row, prev_gate, hid_sems.at[2], hid_sems.at[3], {"section": after})
     out_copies = [
         pltpu.make_async_copy(out_hbm.at[index], w_out.at[index], sem_out.at[index])
         for index in range(n)
@@ -312,15 +309,6 @@
         fresh_stage[index] = jnp.where(
             is_key, all_f32[0, span, :][:, None, :], all_f32[1, span, :][:, None, :]
         ).astype(bf16)
-    own_fresh = pltpu.make_async_copy(
-        fresh_stage.at[me], fresh_hbm.at[0, :, :, cols_of(me)], sem_small.at[6]
-    )
-    own_fresh.start()
-    for step in range(1, n):
-        send(
-            fresh_stage.at[peer(step)], fresh_hbm.at[0, :, :, cols_of(me)],
-            fresh_s.at[step], fresh_r.at[me], {"seq": peer(step)},
-        )
     arrivals(1, value_s, value_r)
     for place, (first, last) in enumerate(cuts):
         if place > 0:
@@ -336,8 +324,6 @@
         for step in range(1, n):
             send(piece, piece, att_s.at[place, step], att_r.at[place, me], {"seq": peer(step)})
 
-    gate = jnp.sum(jnp.where(chosen, mod[2, :, cols_of(me)], 0.0), axis=0, keepdims=True)
-
     for copy in out_copies:
         copy.wait()
     total = jnp.dot(att_buf[me], w_out[me], preferred_element_type=f32)
@@ -348,22 +334,29 @@
                 att_buf.at[source, :, pl.ds(first, last - first)],
                 att_s.at[place, step], att_r.at[place, source], {"seq": source},
             )
+            if place == len(cuts) - 1 and step == n - 1:
+                own_fresh = pltpu.make_async_copy(
+                    fresh_stage.at[me], fresh_hbm.at[0, :, :, cols_of(me)], sem_small.at[6]
+                )
+                own_fresh.start()
+                for other in range(1, n):
+                    send(
+                        fresh_stage.at[peer(other)], fresh_hbm.at[0, :, :, cols_of(me)],
+                        fresh_s.at[other], fresh_r.at[me], {"seq": peer(other)},
+                    )
             total += jnp.dot(
                 att_buf[source, :, first:last], w_out[source, first:last, :],
                 preferred_element_type=f32,
             )
-    for step in range(1, n):
-        source = origin(step)
-        arrival(hid_cols.at[source], hid_s.at[step], hid_r.at[source], {"seq": source})
-    change = gate * total.astype(bf16).astype(f32)
     for index in range(n):
-        block = hid_cols[index].astype(f32) + change[index * tokens : (index + 1) * tokens]
-        block_stage[index] = block.astype(bf16)
+        block_stage[index] = total[index * tokens : (index + 1) * tokens].astype(bf16)
     for index in range(n):
         send(
-            block_stage.at[index], next_hbm.at[0, :, cols_of(me)],
-            blk_s.at[index], blk_r.at[me], {"section": after, "seq": index},
-        )
+            block_stage.at[index], landed.at[me], blk_s.at[index], blk_r.at[me],
+            {"section": after, "seq": index},
+        )
+    arrival(prev_rows, hid_sems.at[0], hid_sems.at[1], {"section": before})
+    arrival(prev_gate, hid_sems.at[2], hid_sems.at[3], {"section": before})
     own_fresh.wait()
     for step in range(1, n):
         source = origin(step)
@@ -372,10 +365,10 @@
             {"seq": source},
         )
     for index in range(n):
-        arrival(
-            next_hbm.at[0, :, cols_of(index)], blk_s.at[index], blk_r.at[index],
-            {"section": before, "seq": index},
-        )
+        arrival(landed.at[index], blk_s.at[index], blk_r.at[index], {"section": before, "seq": index})
+        span = slice(index * cols, (index + 1) * cols)
+        change = prev_gate[:, span] * landed[index].astype(f32)
+        next_ref[0, :, span] = (prev_rows[:, span].astype(f32) + change).astype(bf16)
     for copy in sends:
         copy.wait_send()
 
@@ -404,9 +397,12 @@
             pltpu.VMEM((1, tokens, 2, width), bf16),
         ),
         in_specs=[in_hbm] * 8,
-        out_specs=(anywhere, anywhere),
+        out_specs=(pl.BlockSpec(memory_space=pltpu.VMEM), anywhere),
         scratch_shapes=[
             pltpu.VMEM((tokens, width), bf16),
+            pltpu.VMEM((tokens, width), bf16),
+            pltpu.VMEM((1, width), f32),
+            pltpu.VMEM((1, width), f32),
             pltpu.VMEM((n, tokens, cols), bf16),
             pltpu.VMEM((n, tokens, width), bf16),
             pltpu.VMEM((rows, width), f32),
@@ -429,7 +425,8 @@
             dma((parts, n)),
             dma((parts, n)),
         ]
-        + [dma((n,))] * 8
+        + [dma((4,))]
+        + [dma((n,))] * 6
         + [dma((len(cuts), n))] * 2
         + [dma((n,))] * 2,
         compiler_params=pltpu.CompilerParams(

time: 24.1 us -> 23.8 us (0.988); the launches traced: 23.9 us -> 23.4 us
  Pallas kernels: 22.1 us -> 21.5 us
    pallas_call x1, Pallas kernels: 22.1 us -> 21.5 us  [fused(): pl.pallas_call(functools.partial(fused_kernel, n, sections, chunk, cuts),...]
where the time goes in v7:
time: 23.8 us; the launch traced here: 23.4 us
  Pallas kernels  21.5 us (90%)
  local copies, waits for them, and re-layouts  1.23 us (5%)
  between operations  0.64 us (3%)
    pallas_call x1, Pallas kernels, fused(): pl.pallas_call(functools.partial(fused_kernel, n, sections, chunk, cuts),...  21.5 us
    unnamed x2, local copies, waits for them, and re-layouts  1.23 us

profile of v7, /device:TPU:1, one launch (start us, length us, event | category | flops | bytes accessed | tf_op | source)
XLA Modules:
  0.0 23.4 jit_solution(14282689383730722769)
XLA Ops:
  0.6 21.5 %shard_map.95 = (bf16[1,4,3072]{2,1,0:T(4,128)(2,1)S(1)}, bf16[1,4,2,3072]{3,2,1,0:T(2,128)(2,1)S(1)}) custom-call(s32[4]{0:T(128)} %patch_hbm.1, s32[4]{0:T(128)} %step_hbm.1, bf16[1,4,3072]{2,1,0:T(4,128)(2,1)} %hidden_hbm.1, bf16[1,4,4,2,3072]{4,3,2,1,0:T(2,128)(2,1)} %cache_hbm.1, bf16[3,3072,768]{2,1,0:T(8,128)(2,1)} %bitcast.7, ...), custom_call_target="tpu_custom_call" | custom-call | tf_op jit(solution)/shard_map/pallas_call | solution.py:393
  22.2 0.6 %copy.12 = bf16[1,4,3072]{2,1,0:T(4,128)(2,1)} copy(bf16[1,4,3072]{2,1,0:T(4,128)(2,1)S(1)} %get-tuple-element.2) | data formatting | bytes 49152
  22.8 0.6 %copy.13 = bf16[1,4,2,3072]{3,2,1,0:T(2,128)(2,1)} copy(bf16[1,4,2,3072]{3,2,1,0:T(2,128)(2,1)S(1)} %get-tuple-element.3) | data formatting | bytes 98304
